TPU v7x, 32 devices: a whole 2x2x4 slice. The times are simulated.
32 devices in a mesh: rep: 8 (over y, x, core), shard: 4 (over z).
Axes of the slice: x: 2, y: 2, z: 4, core: 2. Of those that a mesh axis runs over, the one named last changes fastest.
Arguments:
- prompt_in: bfloat16 [8, 1024, 2048], P('rep', 'shard'), may hold values from -6 to 6
- cont_in: bfloat16 [8, 8, 96, 2048], P('rep', 'shard'), may hold values from -6 to 6
- cotan_prompt: bfloat16 [8, 1024, 2048], P('rep', 'shard'), may hold values from -6 to 6
- cotan_cont: bfloat16 [8, 8, 96, 2048], P('rep', 'shard'), may hold values from -6 to 6
- routes_attn_p: int32 [8, 1024, 2], P('rep', 'shard'), may hold values from 0 to 3, all different within a row; in each aligned block of 256 rows (0 to 255, 256 to 511, ..., all dimensions but the last counted through in order) at most 136 rows name the same one
- routes_attn_c: int32 [8, 8, 96, 2], P('rep', 'shard'), may hold values from 0 to 3, all different within a row; in each aligned block of 192 rows (0 to 191, 192 to 383, ..., all dimensions but the last counted through in order) at most 104 rows name the same one
- routes_ffn_p: int32 [8, 1024, 2], P('rep', 'shard'), may hold values from 0 to 3, all different within a row; in each aligned block of 256 rows (0 to 255, 256 to 511, ..., all dimensions but the last counted through in order) at most 136 rows name the same one
- routes_ffn_c: int32 [8, 8, 96, 2], P('rep', 'shard'), may hold values from 0 to 3, all different within a row; in each aligned block of 192 rows (0 to 191, 192 to 383, ..., all dimensions but the last counted through in order) at most 104 rows name the same one
- adapter_pick: int32 [8], P('rep'), may hold values from 0 to 7
- norm_gains: bfloat16 [2, 2048], replicated, may hold values from 0.5 to 1.5
- router_attn: bfloat16 [2048, 4], replicated, may hold values from -0.09375 to 0.09375
- router_ffn: bfloat16 [2048, 4], replicated, may hold values from -0.09375 to 0.09375
- w_kv: bfloat16 [2, 2048, 2048], P(None, None, 'shard'), may hold values from -0.125 to 0.125
- w_query: bfloat16 [4, 2048, 2048], P(None, None, 'shard'), may hold values from -0.125 to 0.125
- w_out: bfloat16 [4, 2048, 2048], P(None, None, 'shard'), may hold values from -0.5 to 0.5
- w_gate_up: bfloat16 [4, 2, 2048, 5632], P(None, None, None, 'shard'), may hold values from -0.125 to 0.125
- w_down: bfloat16 [4, 5632, 2048], P(None, 'shard'), may hold values from -0.078125 to 0.078125
- ada_in: bfloat16 [8, 6, 16, 2048], P(None, None, None, 'shard'), may hold values from -0.125 to 0.125
- ada_out: bfloat16 [8, 5, 16, 2048], P(None, None, None, 'shard'), may hold values from -0.75 to 0.75
- ada_down: bfloat16 [8, 16, 5632], P(None, None, 'shard'), may hold values from -0.078125 to 0.078125
- ada_ffn: bfloat16 [8, 2, 16, 5632], P(None, None, None, 'shard'), may hold values from -0.75 to 0.75
Outputs:
- out_prompt: bfloat16 [8, 1024, 2048], P('rep', 'shard')
- out_cont: bfloat16 [8, 8, 96, 2048], P('rep', 'shard')
- grad_prompt: float32 [8, 1024, 2048], P('rep', 'shard')
- grad_cont: float32 [8, 8, 96, 2048], P('rep', 'shard')
- grad_ada_in: float32 [8, 6, 16, 2048], P(None, None, None, 'shard')
- grad_ada_out: float32 [8, 5, 16, 2048], P(None, None, None, 'shard')
- grad_ada_down: float32 [8, 16, 5632], P(None, None, 'shard')
- grad_ada_ffn: float32 [8, 2, 16, 5632], P(None, None, None, 'shard')
Inputs may be any that keep to these rules, and one draw needn't show every extreme that they name: `routes_attn_p`: in each aligned block of 256 prompt rows, no attention expert is named by more than 136 rows, a bound that some block reaches; a row names 2 different experts. `routes_attn_c`: in each aligned block of 192 continuation rows, no attention expert is named by more than 104 rows, a bound that some block reaches; a row names 2 different experts. `routes_ffn_p`: in each aligned block of 256 prompt rows, no feed-forward expert is named by more than 136 rows, a bound that some block reaches; a row names 2 different experts. `routes_ffn_c`: in each aligned block of 192 continuation rows, no feed-forward expert is named by more than 104 rows, a bound that some block reaches; a row names 2 different experts.
All inputs are finite; a program needn't handle non-finite values.
Results may differ from a plain program's by a relative error of at most 0.019.
Values may be sent and summed in bfloat16 or wider, within the bound.
No kernel may reach another device: no remote copies, remote signals or barrier semaphores. Data moves between devices by JAX's collectives and lax.ppermute only.
A program may use at most 960 MiB of HBM per device.

v0:
```python
import functools

import jax
import jax.numpy as jnp
from jax import lax
from jax.experimental import pallas as pl
from jax.experimental.pallas import tpu as pltpu
from jax.sharding import PartitionSpec as P

HD = 128
SCALE = HD**-0.5
EPSILON = 1e-05
HIGHEST = lax.Precision.HIGHEST
F32 = jnp.float32
BF16 = jnp.bfloat16
EXT = 128


def dot32(former, latter):
    return jnp.dot(former, latter, preferred_element_type=F32)


def dot_nt(former, latter):
    return lax.dot_general(former, latter, (((1,), (1,)), ((), ())), preferred_element_type=F32)


def dot_tn(former, latter):
    return lax.dot_general(former, latter, (((0,), (0,)), ((), ())), preferred_element_type=F32)


def exact_mm(former, latter):
    return jnp.dot(former, latter, precision=HIGHEST)


def split_low(values):
    high = values.astype(BF16)
    return [high, (values - high.astype(F32)).astype(BF16)]


def twice(values):
    return jnp.concatenate([values, values], axis=0)


def norm_rows(values, scaling):
    inverse = lax.rsqrt(jnp.mean(values * values, axis=-1, keepdims=True) + EPSILON)
    return (values * inverse * scaling, inverse)


def norm_back(values, inverse, scaling, upstream):
    weighted = upstream * scaling
    inner_mean = jnp.mean(weighted * values, axis=-1, keepdims=True)
    return inverse * weighted - values * (inverse * inverse * inverse) * inner_mean


def capacity(block_rows, experts, top_count):
    return min(block_rows, ((block_rows * top_count + experts - 1) // experts + 7) // 8 * 8 + 8)


def hits(routes, experts):
    labels = jnp.arange(experts, dtype=jnp.int32)
    return (routes[:, :, None] == labels[None, None, :]).astype(F32)


def slot_onehots(routes, experts, block):
    rows, top_count = routes.shape
    slot_cap = capacity(block, experts, top_count)
    member = jnp.sum(hits(routes, experts), axis=1).reshape(-1, 2, block, experts)
    place = jnp.arange(block, dtype=jnp.int32)
    before = (place[None, :] < place[:, None]).astype(BF16)
    ranked = jnp.einsum("rq,phqe->phre", before, member.astype(BF16), preferred_element_type=F32)
    ranked = ranked + jnp.arange(2, dtype=F32)[None, :, None, None] * slot_cap
    slot_of = jnp.where(member > 0, ranked, -1.0).reshape(-1, 2 * block, experts)
    slots = jnp.arange(2 * slot_cap, dtype=F32)
    return (slot_of.transpose(2, 0, 1)[:, :, None, :] == slots[None, None, :, None]).astype(BF16)


def route_shares(logits, routes):
    chosen = jnp.einsum("rte,re->rt", hits(routes, logits.shape[1]), logits, precision=HIGHEST)
    return jax.nn.softmax(chosen, axis=-1)


def shares_back(shares, routes, experts, d_shares):
    d_chosen = shares * (d_shares - jnp.sum(shares * d_shares, axis=-1, keepdims=True))
    return jnp.sum(d_chosen[:, :, None] * hits(routes, experts), axis=1)


def with_ext(rows, columns):
    used = sum(c.shape[1] for c in columns)
    columns = [c.astype(BF16) for c in columns]
    blank = jnp.zeros((rows.shape[0], EXT - used), BF16)
    return jnp.concatenate([rows.astype(BF16)] + columns + [blank], axis=1)


def whole(*shape):
    return pl.BlockSpec(
        shape, lambda *ids: (0,) * len(shape), pipeline_mode=pl.Buffered(buffer_count=1)
    )


def anywhere():
    return pl.BlockSpec(memory_space=pl.ANY)


def kernel_params(dims, mib):
    return pltpu.CompilerParams(
        dimension_semantics=("arbitrary",) * dims, vmem_limit_bytes=mib * 2**20
    )


def pair_rows(ref, span):
    start, rows = span
    return ref[:, start : start + rows, :].reshape(2 * rows, ref.shape[2])


def ext_choice(ext, tops, experts, rank):
    ext = ext[...].astype(F32)
    at = 3 * rank
    shares = [ext[:, at + t : at + t + 1] + ext[:, at + tops + t : at + tops + t + 1] for t in range(tops)]
    at = at + 2 * tops
    chosen = [[ext[:, at + t : at + t + 1] == e for e in range(experts)] for t in range(tops)]
    return shares, chosen


def qkv_kernel(span, tops, rank, load, routes, w_q, w_kv, fac_a, fac_b, q, k, v, low_out):
    features = w_q.shape[1]
    experts = w_q.shape[0]
    rows = span[1]
    block = pair_rows(load, span)
    n1 = block
    route = pair_rows(routes, span)[:, :tops].astype(F32)
    chosen = [[route[:, t : t + 1] == e for e in range(experts)] for t in range(tops)]
    low = dot_nt(n1, fac_a[...])
    logits = [
        sum(jnp.where(chosen[t][e], low[:, 3 * rank + e : 3 * rank + e + 1], 0.0) for e in range(experts))
        for t in range(tops)
    ]
    peak = functools.reduce(jnp.maximum, logits)
    shares = [jnp.exp(m - peak) for m in logits]
    total = sum(shares)
    shares = split_low(jnp.concatenate([m / total for m in shares], axis=1))
    low_out[...] = jnp.concatenate(
        [low[:, : 3 * rank].astype(BF16)]
        + shares
        + [route.astype(BF16), jnp.zeros((2 * rows, EXT - 3 * rank - 3 * tops), BF16)],
        axis=1,
    )
    shift = []
    for j in range(3):
        wide = jnp.concatenate(split_low(low[:, rank * j : rank * (j + 1)]), axis=1)
        shift.append(dot32(wide, twice(fac_b[j])))
    k[...] = (dot32(n1, w_kv[0]) + shift[1]).astype(BF16)
    v[...] = (dot32(n1, w_kv[1]) + shift[2]).astype(BF16)
    picked = [shift[0]] * tops
    for e in range(experts):
        here = dot32(n1, w_q[e])
        for t in range(tops):
            picked[t] = picked[t] + jnp.where(chosen[t][e], here, 0.0)
    for t in range(tops):
        q[t] = picked[t].astype(BF16)


def qkv_call(load, routes, span, tops, w_q, w_kv, fac_a, fac_b):
    shards, held, wide = load.shape
    rows = span[1]
    width = w_q.shape[2]
    total = shards * rows
    rank = fac_b.shape[1]
    out = lambda n: pl.BlockSpec((2 * rows, n), lambda p: (p, 0))
    return pl.pallas_call(
        functools.partial(qkv_kernel, span, tops, rank),
        grid=(shards // 2,),
        in_specs=[
            pl.BlockSpec((2, held, wide), lambda p: (p, 0, 0)),
            pl.BlockSpec((2,) + routes.shape[1:], lambda p: (p, 0, 0)),
            whole(*w_q.shape),
            whole(*w_kv.shape),
            whole(*fac_a.shape),
            whole(*fac_b.shape),
        ],
        out_specs=[
            pl.BlockSpec((tops, 2 * rows, width), lambda p: (0, p, 0)),
            out(width),
            out(width),
            out(EXT),
        ],
        out_shape=[
            jax.ShapeDtypeStruct((tops, total, width), BF16),
            jax.ShapeDtypeStruct((total, width), BF16),
            jax.ShapeDtypeStruct((total, width), BF16),
            jax.ShapeDtypeStruct((total, EXT), BF16),
        ],
        compiler_params=kernel_params(1, 56),
        cost_estimate=pl.CostEstimate(
            flops=2 * total * w_q.shape[1] * width * (w_q.shape[0] + 2),
            bytes_accessed=2 * (w_q.size + w_kv.size + load.size),
            transcendentals=0,
        ),
        name="qkv",
    )(load, routes, w_q, w_kv, fac_a, fac_b)


def out_kernel(tops, ext, o, w_o, fac_a, fac_b, out):
    experts = w_o.shape[0]
    shares, chosen = ext_choice(ext, tops, experts, fac_a.shape[0])
    parts = [o[t].astype(F32) * shares[t] for t in range(tops)]
    low = dot_nt(sum(parts).astype(BF16), fac_a[...])
    total = dot32(jnp.concatenate(split_low(low), axis=1), twice(fac_b[...]))
    for e in range(experts):
        here = sum(jnp.where(chosen[t][e], parts[t], 0.0) for t in range(tops)).astype(BF16)
        total = total + dot32(here, w_o[e])
    out[...] = total.astype(BF16)


def out_call(ext, rows, o, w_o, fac_a, fac_b):
    tops, total, width = o.shape
    features = w_o.shape[2]
    return pl.pallas_call(
        functools.partial(out_kernel, tops),
        grid=(total // (2 * rows),),
        in_specs=[
            pl.BlockSpec((2 * rows, EXT), lambda p: (p, 0)),
            pl.BlockSpec((tops, 2 * rows, width), lambda p: (0, p, 0)),
            whole(*w_o.shape),
            whole(*fac_a.shape),
            whole(*fac_b.shape),
        ],
        out_specs=pl.BlockSpec((2 * rows, features), lambda p: (p, 0)),
        out_shape=jax.ShapeDtypeStruct((total, features), BF16),
        compiler_params=kernel_params(1, 56),
        cost_estimate=pl.CostEstimate(
            flops=2 * total * w_o.size,
            bytes_accessed=2 * (w_o.size + o.size + total * features),
            transcendentals=0,
        ),
        name="project_out",
    )(ext, o, w_o, fac_a, fac_b)


def out_back_kernel(tops, ext, dh, o, w_o, fac_a, fac_b, do, dw, grad_a, grad_b):
    experts = w_o.shape[0]
    shares, chosen = ext_choice(ext, tops, experts, fac_a.shape[0])
    block = dh[...].reshape(-1, dh.shape[2])
    rows = block.shape[0]
    low = split_low(dot_nt(block, fac_b[...]))
    shift = dot32(jnp.concatenate(low, axis=1), twice(fac_a[...]))
    picked = [shift] * tops
    for e in range(experts):
        here = dot_nt(block, w_o[e])
        for t in range(tops):
            picked[t] = picked[t] + jnp.where(chosen[t][e], here, 0.0)
    lane = lax.broadcasted_iota(jnp.int32, (rows, EXT), 1)
    back = jnp.zeros((rows, EXT), F32)
    total = None
    for t in range(tops):
        value = o[t].astype(F32)
        back = back + jnp.where(lane == t, jnp.sum(picked[t] * value, axis=1, keepdims=True), 0.0)
        do[t] = (picked[t] * shares[t]).astype(BF16)
        value = value * shares[t]
        total = value if total is None else total + value
    dw[...] = back.astype(BF16)
    total = total.astype(BF16)

    @pl.when(pl.program_id(0) == 0)
    def _():
        grad_a[...] = jnp.zeros_like(grad_a)
        grad_b[...] = jnp.zeros_like(grad_b)

    grad_a[...] += dot_tn(low[0], total)
    grad_b[...] += dot_tn(dot_nt(total, fac_a[...]).astype(BF16), block)


def out_back_call(ext, rows, dh, o, w_o, fac_a, fac_b):
    tops, total, width = o.shape
    rank, features = fac_b.shape
    two = pl.BlockSpec((tops, 2 * rows, width), lambda p: (0, p, 0))
    row = pl.BlockSpec((2 * rows, EXT), lambda p: (p, 0))
    return pl.pallas_call(
        functools.partial(out_back_kernel, tops),
        grid=(total // (2 * rows),),
        in_specs=[
            row,
            pl.BlockSpec((2,) + dh.shape[1:], lambda p: (p, 0, 0)),
            two,
            whole(*w_o.shape),
            whole(*fac_a.shape),
            whole(*fac_b.shape),
        ],
        out_specs=[
            two,
            row,
            pl.BlockSpec((rank, width), lambda p: (0, 0)),
            pl.BlockSpec((rank, features), lambda p: (0, 0)),
        ],
        out_shape=[
            jax.ShapeDtypeStruct(o.shape, BF16),
            jax.ShapeDtypeStruct((total, EXT), BF16),
            jax.ShapeDtypeStruct((rank, width), F32),
            jax.ShapeDtypeStruct((rank, features), F32),
        ],
        compiler_params=kernel_params(1, 56),
        cost_estimate=pl.CostEstimate(
            flops=2 * total * w_o.size,
            bytes_accessed=2 * (w_o.size + 2 * o.size + total * features),
            transcendentals=0,
        ),
        name="project_out_back",
    )(ext, dh, o, w_o, fac_a, fac_b)


def qkv_back_kernel(span, tops, rank, load, dq, dk, dv, low_in, w_q, w_kv, fac_b, fac_a, out, grad_a, grad_b):
    experts, features, _ = w_q.shape
    rows = span[1]
    block = pair_rows(load, span)
    _, chosen = ext_choice(low_in, tops, experts, rank)
    total = dot_nt(dk[...], w_kv[0]) + dot_nt(dv[...], w_kv[1])
    blank = jnp.zeros(dk.shape, BF16)
    for e in range(experts):
        here = blank
        for t in range(tops):
            here = jnp.where(chosen[t][e], dq[t], here)
        total = total + dot_nt(here, w_q[e])
    dq_sum = sum(dq[t].astype(F32) for t in range(tops)).astype(BF16)
    sides = [dq_sum, dk[...], dv[...]]
    low = jnp.concatenate([dot_nt(sides[j], fac_b[j]) for j in range(3)], axis=1)
    total = total + dot32(jnp.concatenate(split_low(low), axis=1), twice(fac_a[...]))
    out[...] = total.astype(BF16)

    @pl.when(pl.program_id(0) == 0)
    def _():
        grad_a[...] = jnp.zeros_like(grad_a)
        grad_b[...] = jnp.zeros_like(grad_b)

    grad_a[...] += dot_tn(low.astype(BF16), block)
    for j in range(3):
        grad_b[j] += dot_tn(low_in[:, rank * j : rank * (j + 1)], sides[j])


def qkv_back_call(load, span, dq, dk, dv, low_in, w_q, w_kv, fac_b, fac_a, earlier):
    tops, total, width = dq.shape
    rows = span[1]
    features = w_q.shape[1]
    rank = fac_b.shape[1]
    row = lambda n: pl.BlockSpec((2 * rows, n), lambda p: (p, 0))

    def kernel(*refs):
        qkv_back_kernel(span, tops, rank, *refs[:9], *refs[9 + len(earlier) :])

    return pl.pallas_call(
        kernel,
        grid=(total // (2 * rows),),
        in_specs=[
            pl.BlockSpec((2,) + load.shape[1:], lambda p: (p, 0, 0)),
            pl.BlockSpec((tops, 2 * rows, width), lambda p: (0, p, 0)),
            row(width),
            row(width),
            row(EXT),
            whole(*w_q.shape),
            whole(*w_kv.shape),
            whole(*fac_b.shape),
            whole(*fac_a.shape),
        ]
        + [anywhere() for _ in earlier],
        out_specs=[
            row(features),
            pl.BlockSpec((3 * rank, features), lambda p: (0, 0)),
            pl.BlockSpec((3, rank, width), lambda p: (0, 0, 0)),
        ],
        out_shape=[
            jax.ShapeDtypeStruct((total, features), BF16),
            jax.ShapeDtypeStruct((3 * rank, features), F32),
            jax.ShapeDtypeStruct((3, rank, width), F32),
        ],
        compiler_params=kernel_params(1, 56),
        cost_estimate=pl.CostEstimate(
            flops=2 * total * (w_q.size + w_kv.size),
            bytes_accessed=2 * (w_q.size + w_kv.size + 2 * load.size),
            transcendentals=0,
        ),
        name="qkv_back",
    )(load, dq, dk, dv, low_in, w_q, w_kv, fac_b, fac_a, *earlier)


def ffn_tiles(units):
    if units % 128:
        return [(0, units)]
    return [(start, min(512, units - start)) for start in range(0, units, 512)]


def ffn_kernel(tiles, rank, begin, hot, n2, c, w_gu, w_d, fac_gu, fac_d, y_out, dx_out, g_out, xs, cs, acc_y, acc_d, buf_gu, buf_d, sems):
    e = pl.program_id(0)
    here = pl.num_programs(0)
    experts, _, features = w_d.shape
    count = len(tiles)
    pairs, slots, _ = hot.shape[1:]
    rows = n2.shape[1]
    total = pairs * slots
    side = pl.ds(features, EXT)

    def copies(expert, t, slot):
        start, size = tiles[t]
        cols = pl.ds(start, size)
        got = pl.ds(0, size)
        pairs_of = [
            (w_gu.at[begin + expert, 0, :, cols], buf_gu.at[slot, 0, pl.ds(0, features), got]),
            (w_gu.at[begin + expert, 1, :, cols], buf_gu.at[slot, 1, pl.ds(0, features), got]),
            (w_d.at[begin + expert, cols, :], buf_d.at[slot, got, pl.ds(0, features)]),
            (fac_gu.at[:, :, cols], buf_gu.at[slot, :, side, got]),
            (fac_d.at[cols, :], buf_d.at[slot, got, side]),
        ]
        return [pltpu.make_async_copy(*m, sems.at[slot, n]) for n, m in enumerate(pairs_of)]

    @pl.when(e == 0)
    def _():
        for m in copies(0, 0, 0):
            m.start()
        g_out[...] = jnp.zeros_like(g_out)

    for p in range(pairs):
        spot = pl.ds(p * slots, slots)
        xs[spot, :] = dot32(hot[0, p], n2[2 * p : 2 * p + 2].reshape(2 * rows, -1)).astype(BF16)
        cs[spot, :] = dot32(hot[0, p], c[2 * p : 2 * p + 2].reshape(2 * rows, -1)).astype(BF16)
    lane = lax.broadcasted_iota(jnp.int32, (total, EXT), 1)
    ext = xs[:, features:]
    mine = (lane == 4 * rank + begin + e) | (lane == 4 * rank + experts + begin + e)
    share = jnp.sum(jnp.where(mine, ext.astype(F32), 0.0), axis=1, keepdims=True)
    low = [ext[:, :rank], ext[:, 2 * rank : 3 * rank], cs[:, features : features + rank]]
    low[2] = (low[2].astype(F32) * share).astype(BF16)
    dw = None
    for t, (start, size) in enumerate(tiles):
        slot = lax.rem(e * count + t, 2)
        for m in copies(e, t, slot):
            m.wait()
        if t + 1 < count:
            for m in copies(e, t + 1, 1 - slot):
                m.start()
        else:

            @pl.when(e + 1 < here)
            def _():
                for m in copies(e + 1, 0, 1 - slot):
                    m.start()

        spot = pl.ds(0, size)
        cols = pl.ds(start, size)
        wg, wu, wd = buf_gu.at[slot, 0, :, spot], buf_gu.at[slot, 1, :, spot], buf_d.at[slot, spot, :]
        g0 = dot32(xs[...], wg[...])
        g1 = dot32(xs[...], wu[...])
        da = dot_nt(cs[...], wd[...])
        sig = 1.0 / (1.0 + jnp.exp(-g0))
        silu = g0 * sig
        act = (silu * g1).astype(BF16)
        now = jnp.sum(da * act.astype(F32), axis=1, keepdims=True)
        dw = now if dw is None else dw + now
        da = da * share
        dg0 = (da * g1 * (sig + silu * (1.0 - sig))).astype(BF16)
        dg1 = (da * silu).astype(BF16)
        g_out[0, :, cols] += dot_tn(low[0], dg0)
        g_out[1, :, cols] += dot_tn(low[1], dg1)
        g_out[2, :, cols] += dot_tn(low[2], act)
        if t == 0 and count > 1:
            acc_y[...] = dot32(act, wd[...])
            acc_d[...] = dot_nt(dg0, wg[...]) + dot_nt(dg1, wu[...])
        elif t + 1 < count:
            acc_y[...] += dot32(act, wd[...])
            acc_d[...] += dot_nt(dg0, wg[...]) + dot_nt(dg1, wu[...])
        else:
            y = dot32(act, wd[...])
            d = dot_nt(dg0, wg[...]) + dot_nt(dg1, wu[...])
            if count > 1:
                y, d = y + acc_y[...], d + acc_d[...]
            y_out[0] = (y * share).astype(BF16)
            dx_out[0] = d.astype(BF16)
            d = jnp.where(lane == 4 * rank + begin + e, dw, d[:, features:])
            dx_out[0, :, features:] = d.astype(BF16)


def ffn_call(hot, n2, c, w_gu, w_d, fac_gu, fac_d, rank, earlier, begin, experts):
    _, pairs, slots, _ = hot.shape
    total = pairs * slots
    units, features = w_d.shape[1:]
    wide = features + EXT
    tiles = ffn_tiles(units)
    widest = max(size for _, size in tiles)
    one = lambda *s: pl.BlockSpec((1,) + s, lambda e: (e,) + (0,) * len(s))

    def kernel(*refs):
        ffn_kernel(tiles, rank, begin, *refs[:7], *refs[8:])

    return pl.pallas_call(
        kernel,
        grid=(experts,),
        in_specs=[
            pl.BlockSpec((1,) + hot.shape[1:], lambda e: (begin + e, 0, 0, 0)),
            whole(*n2.shape),
            whole(*c.shape),
        ]
        + [anywhere() for _ in range(5)],
        out_specs=[
            one(total, wide),
            one(total, wide),
            pl.BlockSpec((3, rank, units), lambda e: (0, 0, 0)),
        ],
        out_shape=[
            jax.ShapeDtypeStruct((experts, total, wide), BF16),
            jax.ShapeDtypeStruct((experts, total, wide), BF16),
            jax.ShapeDtypeStruct((3, rank, units), F32),
        ],
        scratch_shapes=[
            pltpu.VMEM((total, wide), BF16),
            pltpu.VMEM((total, wide), BF16),
            pltpu.VMEM((total, wide), F32),
            pltpu.VMEM((total, wide), F32),
            pltpu.VMEM((2, 2, wide, widest), BF16),
            pltpu.VMEM((2, widest, wide), BF16),
            pltpu.SemaphoreType.DMA((2, 5)),
        ],
        compiler_params=kernel_params(1, 62),
        cost_estimate=pl.CostEstimate(
            flops=12 * experts * total * features * units,
            bytes_accessed=6 * experts * features * units + 8 * experts * total * features,
            transcendentals=experts * total * units,
        ),
        name="ffn",
    )(hot, n2, c, w_gu, w_d, fac_gu, fac_d, earlier)


def rows_call(hot, parts, source, fac, lows, keep, earlier):
    experts, pairs, slots, rows = hot.shape
    count, _, wide = parts[0].shape
    rank = fac.shape[0] // len(lows)
    features = wide - EXT
    parts = [m.reshape(count, pairs, slots, wide) for m in parts]
    by_pair = lambda n, *s: pl.BlockSpec((n, 1) + s, lambda p: (0, p, 0, 0))

    def kernel(hot, *refs):
        values, source, fac, _, out, grad = refs[: len(parts)], *refs[len(parts) :]
        total = None
        for e in range(experts):
            here = dot_tn(hot[e, 0], values[e // count][e % count, 0])
            total = here if total is None else total + here
        low = [total[:, features + at : features + at + rank] for at in lows]
        low = split_low(jnp.concatenate(low, axis=1))
        main = total[:, :features] + dot32(jnp.concatenate(low, axis=1), twice(fac[...]))
        out[:, :features] = main.astype(BF16)
        if keep:
            out[:, features:] = total[:, features:].astype(BF16)

        @pl.when(pl.program_id(0) == 0)
        def _():
            grad[...] = jnp.zeros_like(grad)

        grad[...] += dot_tn(low[0], source[:, :, :features].reshape(rows, features))

    out_wide = wide if keep else features
    return pl.pallas_call(
        kernel,
        grid=(pairs,),
        in_specs=[by_pair(experts, slots, rows)]
        + [by_pair(count, slots, wide) for _ in parts]
        + [
            pl.BlockSpec((2,) + source.shape[1:], lambda p: (p, 0, 0)),
            whole(*fac.shape),
            anywhere(),
        ],
        out_specs=[
            pl.BlockSpec((rows, out_wide), lambda p: (p, 0)),
            pl.BlockSpec(fac.shape, lambda p: (0, 0)),
        ],
        out_shape=[
            jax.ShapeDtypeStruct((pairs * rows, out_wide), BF16),
            jax.ShapeDtypeStruct(fac.shape, F32),
        ],
        compiler_params=kernel_params(1, 56),
        cost_estimate=pl.CostEstimate(
            flops=2 * hot.size * wide,
            bytes_accessed=2 * (hot.size + experts * pairs * slots * wide),
            transcendentals=0,
        ),
        name="slots_to_rows",
    )(hot, *parts, source, fac, earlier)


def whole_rows(q):
    return q.reshape(q.shape[0]*q.shape[1], q.shape[2])

def masked_pair(q, keys, diag_keys, seen):
    far = None if keys is None else dot_nt(q, keys)
    near = jnp.where(seen, dot_nt(q, diag_keys), -1e30)
    return far, near

def soft_pair(far, near):
    top = jnp.max(near, axis=1, keepdims=True)
    if far is not None: top = jnp.maximum(top, jnp.max(far, axis=1, keepdims=True))
    p_near = jnp.exp((near - top) * SCALE)
    total = jnp.sum(p_near, axis=1, keepdims=True)
    p_far = None
    if far is not None:
        p_far = jnp.exp((far - top) * SCALE)
        total = total + jnp.sum(p_far, axis=1, keepdims=True)
    return p_far, p_near, top * SCALE + jnp.log(total), 1.0 / total

def prompt_seen(tops, size):
    r = lax.broadcasted_iota(jnp.int32, (tops, size, size), 1).reshape(tops*size, size)
    k = lax.broadcasted_iota(jnp.int32, (tops*size, size), 1)
    return k <= r

def cont_seen(tops, size, length):
    r = lax.broadcasted_iota(jnp.int32, (tops, size, size), 1).reshape(tops*size, size)
    k = lax.broadcasted_iota(jnp.int32, (tops*size, size), 1)
    own = k <= r
    for start in range(length, size, length):
        own = own & ((r < start) | (k >= start))
    return own

def forward_tile(q, far_k, far_v, near_k, near_v, seen):
    far, near = masked_pair(q, far_k, near_k, seen)
    p_far, p_near, lse, inv = soft_pair(far, near)
    o = dot32(p_near.astype(BF16), near_v)
    if far is not None: o = o + dot32(p_far.astype(BF16), far_v)
    return (o * inv).astype(BF16), lse

def prompt_fwd(tile, q, k, v, o, lse):
    tops, rows, _ = q.shape
    for start in range(0, rows, tile):
        here = pl.ds(start, tile)
        out, stat = forward_tile(whole_rows(q[:, here, :]), k[:start, :] if start else None, v[:start, :] if start else None, k[here, :], v[here, :], prompt_seen(tops, tile))
        o[:, here, :] = out.reshape(tops, tile, HD)
        lse[0, :, here, :] = stat.reshape(tops, tile, 1)

def cont_fwd(length, q, kp, vp, k, v, earlier, o, lse):
    tops, size, _ = q.shape
    out, stat = forward_tile(whole_rows(q[...]), kp[...], vp[...], k[...], v[...], cont_seen(tops, size, length))
    o[...] = out.reshape(tops, size, HD)
    lse[0] = stat.reshape(tops, size, 1)

def backward_tile(q, do, lse, far_k, far_v, near_k, near_v, seen):
    far, near = masked_pair(q, far_k, near_k, seen)
    p_near = jnp.exp(near * SCALE - lse)
    dp_near = dot_nt(do, near_v)
    delta = jnp.sum(p_near * dp_near, axis=1, keepdims=True)
    if far is not None:
        p_far = jnp.exp(far * SCALE - lse)
        dp_far = dot_nt(do, far_v)
        delta = delta + jnp.sum(p_far * dp_far, axis=1, keepdims=True)
    ds_near = (p_near * (dp_near - delta)).astype(BF16)
    dq = dot32(ds_near, near_k)
    near_grads = dot_tn(ds_near, q) * SCALE, dot_tn(p_near.astype(BF16), do)
    far_grads = None
    if far is not None:
        ds_far = (p_far * (dp_far - delta)).astype(BF16)
        dq = dq + dot32(ds_far, far_k)
        far_grads = dot_tn(ds_far, q) * SCALE, dot_tn(p_far.astype(BF16), do)
    return (dq * SCALE).astype(BF16), far_grads, near_grads

def prompt_bwd(tile, q, k, v, do, lse, dq, dk, dv):
    tops, rows, _ = q.shape
    for start in range(0, rows, tile):
        here = pl.ds(start, tile)
        out, far, near = backward_tile(whole_rows(q[:, here, :]), whole_rows(do[:, here, :]), lse[0, :, here, :].reshape(tops*tile, 1),
            k[:start, :] if start else None, v[:start, :] if start else None, k[here, :], v[here, :], prompt_seen(tops, tile))
        dq[:, here, :] = out.reshape(tops, tile, HD)
        dk[here, :], dv[here, :] = near
        if start:
            dk[:start, :] += far[0]
            dv[:start, :] += far[1]

def cont_bwd(length, q, kp, vp, k, v, do, lse, dkp_in, dvp_in, dq, dkp, dvp, dk, dv, acc_k, acc_v):
    tops, size, _ = q.shape
    step = pl.program_id(1)
    @pl.when(step == 0)
    def _():
        acc_k[...] = dkp_in[...]
        acc_v[...] = dvp_in[...]
    out, far, near = backward_tile(whole_rows(q[...]), whole_rows(do[...]), lse[0].reshape(tops*size, 1), kp[...], vp[...], k[...], v[...], cont_seen(tops, size, length))
    dq[...] = out.reshape(tops, size, HD)
    dk[...], dv[...] = near[0].astype(BF16), near[1].astype(BF16)
    acc_k[...] += far[0]
    acc_v[...] += far[1]
    @pl.when(step == pl.num_programs(1) - 1)
    def _():
        dkp[...] = acc_k[...].astype(BF16)
        dvp[...] = acc_v[...].astype(BF16)

def cost(tops, rows, keys, width, products):
    return pl.CostEstimate(flops=4*tops*rows*keys*width*products, bytes_accessed=8*rows*width*tops, transcendentals=tops*rows*keys*width//HD)

def prompt_specs(tops, rows):
    by_head = pl.BlockSpec((rows, HD), lambda h: (0, h))
    two = pl.BlockSpec((tops, rows, HD), lambda h: (0, 0, h))
    stat = pl.BlockSpec((1, tops, rows, 1), lambda h: (h, 0, 0, 0))
    return by_head, two, stat

def cont_specs(tops, prompt, size):
    keys = pl.BlockSpec((prompt, HD), lambda h, i: (0, h))
    own = pl.BlockSpec((size, HD), lambda h, i: (i, h))
    two = pl.BlockSpec((tops, size, HD), lambda h, i: (0, i, h))
    stat = pl.BlockSpec((1, tops, size, 1), lambda h, i: (h, 0, i, 0))
    return keys, own, two, stat

def attend_prompt(q, k, v, tile=256):
    tops, rows, width = q.shape; heads = width // HD
    by_head, two, stat = prompt_specs(tops, rows)
    return pl.pallas_call(functools.partial(prompt_fwd, tile), grid=(heads,), in_specs=[two, by_head, by_head], out_specs=[two, stat],
        out_shape=[jax.ShapeDtypeStruct(q.shape, BF16), jax.ShapeDtypeStruct((heads, tops, rows, 1), F32)],
        compiler_params=kernel_params(1, 48), cost_estimate=cost(tops, rows, rows//2, width, 1), name="attend_prompt")(q, k, v)

def attend_cont(q, kp, vp, k, v, length, earlier):
    tops, rows, width = q.shape; heads = width // HD; size = 2*length
    keys, own, two, stat = cont_specs(tops, kp.shape[0], size)
    return pl.pallas_call(functools.partial(cont_fwd, length), grid=(heads, rows//size), in_specs=[two, keys, keys, own, own, anywhere()], out_specs=[two, stat],
        out_shape=[jax.ShapeDtypeStruct(q.shape, BF16), jax.ShapeDtypeStruct((heads, tops, rows, 1), F32)],
        compiler_params=kernel_params(2, 48), cost_estimate=cost(tops, rows, kp.shape[0], width, 1), name="attend_cont")(q, kp, vp, k, v, earlier)

def attend_prompt_back(q, k, v, do, lse, tile=256):
    tops, rows, width = q.shape; heads = width // HD
    by_head, two, stat = prompt_specs(tops, rows)
    return pl.pallas_call(functools.partial(prompt_bwd, tile), grid=(heads,), in_specs=[two, by_head, by_head, two, stat], out_specs=[two, by_head, by_head],
        out_shape=[jax.ShapeDtypeStruct(q.shape, BF16)] + [jax.ShapeDtypeStruct(k.shape, F32)]*2,
        compiler_params=kernel_params(1, 48), cost_estimate=cost(tops, rows, rows//2, width, 3), name="attend_prompt_back")(q, k, v, do, lse)

def attend_cont_back(q, kp, vp, k, v, do, lse, dkp, dvp, length):
    tops, rows, width = q.shape; heads = width // HD; size = 2*length
    keys, own, two, stat = cont_specs(tops, kp.shape[0], size)
    return pl.pallas_call(functools.partial(cont_bwd, length), grid=(heads, rows//size), in_specs=[two, keys, keys, own, own, two, stat, keys, keys], out_specs=[two, keys, keys, own, own],
        out_shape=[jax.ShapeDtypeStruct(m.shape, BF16) for m in (q, kp, kp, k, k)], scratch_shapes=[pltpu.VMEM((kp.shape[0], HD), F32)]*2,
        compiler_params=kernel_params(2, 48), cost_estimate=cost(tops, rows, kp.shape[0], width, 3), name="attend_cont_back")(q, kp, vp, k, v, do, lse, dkp, dvp)


def on_device(
    prompt_in,
    cont_in,
    cotan_prompt,
    cotan_cont,
    routes_attn_p,
    routes_attn_c,
    routes_ffn_p,
    routes_ffn_c,
    adapter_pick,
    norm_gains,
    router_attn,
    router_ffn,
    w_kv,
    w_query,
    w_out,
    w_gate_up,
    w_down,
    ada_in,
    ada_out,
    ada_down,
    ada_ffn,
):
    features = prompt_in.shape[2]
    n_attn = w_query.shape[0]
    n_ffn = w_down.shape[0]
    shards = lax.axis_size("shard")
    reps = lax.axis_size("rep")
    rep_id = lax.axis_index("rep")
    shard_id = lax.axis_index("shard")
    hops = range(1, shards)
    cont_len = cont_in.shape[2]
    sizes = (prompt_in.shape[1], cont_in.shape[1] * cont_len)
    width = w_kv.shape[2]
    both = range(2)
    rank = ada_in.shape[2]
    tops = routes_attn_p.shape[2]

    def tie(values, earlier):
        return values + (earlier[(0,) * earlier.ndim] * 0).astype(values.dtype)

    def gather(values):
        return lax.all_gather(values, "shard", axis=0)

    def scatter(values):
        return lax.psum_scatter(values, "shard", scatter_dimension=0, tiled=True)

    def together(former, latter):
        both_of = [m.reshape(shards, -1, m.shape[-1]) for m in (former, latter)]
        return jnp.concatenate(both_of, axis=1).reshape(-1, former.shape[-1])

    def spread_blocks(values):
        block = lambda t: lax.dynamic_index_in_dim(values, t % shards, 0, keepdims=False)
        out = [block(shard_id)]
        for hop in hops:
            pairs = [(k, (k + hop) % shards) for k in range(shards)]
            out.append(lax.ppermute(block(shard_id + hop), "shard", pairs))
        return out

    def in_order(by_distance):
        out = []
        for t in range(shards):
            value = by_distance[0]
            for hop in hops:
                value = jnp.where((shard_id - hop) % shards == t, by_distance[hop], value)
            out.append(value)
        return out

    def cube_gather(values, axis):
        shape, bit, place = values.shape, reps // 2, axis
        while bit:
            other = lax.ppermute(values, "rep", [(k, k ^ bit) for k in range(reps)])
            high = (rep_id // bit) % 2 == 1
            values = jnp.stack(
                [jnp.where(high, other, values), jnp.where(high, values, other)], axis=place
            )
            bit, place = bit // 2, place + 1
        return values.reshape(shape[:axis] + (reps,) + shape[axis:])

    flat = lambda m: m[0].reshape(-1, m.shape[-1])
    x_own = [flat(prompt_in), flat(cont_in)]
    c_own = [flat(cotan_prompt), flat(cotan_cont)]
    ra_own = [flat(routes_attn_p), flat(routes_attn_c)]
    rf_own = [flat(routes_ffn_p), flat(routes_ffn_c)]
    chosen = adapter_pick[0]
    own_in = lax.dynamic_index_in_dim(ada_in, chosen, 0, keepdims=False)
    own_out = lax.dynamic_index_in_dim(ada_out, chosen, 0, keepdims=False)
    own_down = lax.dynamic_index_in_dim(ada_down, chosen, 0, keepdims=False)
    own_ffn = lax.dynamic_index_in_dim(ada_ffn, chosen, 0, keepdims=False)
    gain_one = norm_gains[0].astype(F32)
    gain_two = norm_gains[1].astype(F32)

    factors = jnp.concatenate([own_in[:3], own_in[4:6], own_out[3:5]], axis=0)
    routes = jnp.concatenate([jnp.concatenate(m, axis=0) for m in (ra_own, rf_own)], axis=1)
    extra = jnp.concatenate([factors.reshape(-1), routes.astype(BF16).reshape(-1)])
    extra_rows = -(-extra.size // (16 * features)) * 16
    extra = jnp.pad(extra, (0, extra_rows * features - extra.size)).reshape(extra_rows, features)
    n1_own, r1, wa_own = [], [], []
    for i in both:
        normed, inverse = norm_rows(x_own[i].astype(F32), gain_one)
        normed = normed.astype(BF16)
        n1_own.append(normed)
        r1.append(inverse)
        wa_own.append(route_shares(dot32(normed, router_attn), ra_own[i]))
    sent = jnp.concatenate(n1_own + [extra], axis=0)
    load = gather(sent)
    spans = [(0, sizes[0]), sizes]
    extra = load[:, sum(sizes) :].reshape(shards, -1)
    full = extra[:, : factors.size].reshape((shards,) + factors.shape)
    full = full.transpose(1, 2, 0, 3).reshape(factors.shape[:2] + (-1,))
    a_qkv = jnp.concatenate([full[:3].reshape(3 * rank, features), router_attn.T], axis=0)
    a_ff = full[3:5].reshape(2 * rank, features)
    b_o, b_down = full[5], full[6]
    b_qkv, a_o = own_out[:3], own_in[3]
    routes = extra[:, factors.size : factors.size + routes.size].reshape((shards,) + routes.shape)
    rf = [routes[:, spans[i][0] : sum(spans[i]), tops:].astype(jnp.int32) for i in both]
    rf = [m.reshape(-1, tops) for m in rf]
    hot = [slot_onehots(rf[i], n_ffn, sizes[i]) for i in both]
    routes = jnp.pad(routes, ((0, 0), (0, 0), (0, EXT - 2 * tops)))
    piece = width // reps
    mine = lax.dynamic_index_in_dim(
        w_out.reshape(n_attn, shards, reps, piece, w_out.shape[2]), rep_id, 2, keepdims=False
    )
    turned = spread_blocks(tie(mine.transpose(1, 0, 2, 3), sent))
    turned = jnp.concatenate(in_order(turned), axis=2)
    w_o = cube_gather(turned, 1).reshape(n_attn, width, features)

    q, k, v, low1 = [None, None], [None, None], [None, None], [None, None]
    for i in both:
        q[i], k[i], v[i], low1[i] = qkv_call(load, routes, spans[i], tops, w_query, w_kv, a_qkv, b_qkv)
    o, lse = [None, None], [None, None]
    o[0], lse[0] = attend_prompt(q[0], k[0], v[0])
    c_load = [gather(tie(c_own[0], load))]
    partial = [tie(out_call(low1[0], sizes[0], o[0], w_o, a_o, b_o), c_load[0])]
    o[1], lse[1] = attend_cont(q[1], k[0], v[0], k[1], v[1], cont_len, partial[0])
    partial.append(out_call(low1[1], sizes[1], o[1], w_o, a_o, b_o))
    blank = jnp.zeros((2 * rank, own_down.shape[1]), BF16)
    fac_gu = [twice(own_ffn[0]), blank], [blank, twice(own_ffn[1])]
    fac_gu = jnp.stack([jnp.concatenate(m + [blank] * (EXT // (2 * rank) - 2), axis=0) for m in fac_gu])
    fac_d = jnp.concatenate([twice(own_down)] + [blank] * (EXT // (2 * rank) - 1), axis=0).T
    half = n_ffn // 2
    y_slots, dx, sums = [[], []], [[], []], []

    def run_experts(i, part, earlier):
        one, two, three = ffn_call(
            hot[i],
            n2[i],
            c_load[i],
            w_gate_up,
            w_down,
            fac_gu,
            fac_d,
            rank,
            earlier,
            part * half,
            half,
        )
        y_slots[i].append(one)
        dx[i].append(two)
        sums.append(three)

    def beside_low(rows):
        low = split_low(dot_nt(rows.reshape(-1, features), b_down))
        return with_ext(rows.reshape(-1, features), low).reshape(shards, -1, features + EXT)

    h1, n2_own, r2, wf_own, n2 = [], [], [], [], []
    for i in both:
        if i:
            partial[1] = tie(partial[1], n2[0])
            c_load[0] = beside_low(c_load[0])
            run_experts(0, 0, partial[1])
        hidden = x_own[i].astype(F32) + scatter(partial[i]).astype(F32)
        normed, inverse = norm_rows(hidden, gain_two)
        normed = normed.astype(BF16)
        h1.append(hidden)
        r2.append(inverse)
        n2_own.append(normed)
        wf_own.append(route_shares(dot32(normed, router_ffn), rf_own[i]))
        by_expert = jnp.sum(wf_own[i][:, :, None] * hits(rf_own[i], n_ffn), axis=1)
        low = dot_nt(normed, a_ff)
        columns = split_low(low[:, :rank]) + split_low(low[:, rank:]) + split_low(by_expert)
        n2_sent = with_ext(normed, columns)
        n2_sent = tie(n2_sent, dx[0][0] if i else partial[1])
        n2.append(gather(n2_sent))
    c_last = tie(c_own[1], n2_sent)
    c_load.append(gather(c_last))
    c_load[1] = beside_low(c_load[1])

    dh1, dh_sent, dh_load, d_partial, y_partial, y_own = [], [], [], [], [], []
    g_a_ff, g_b_down = [], []

    def sum_rows(i):
        lows = (0, 2 * rank)
        out, part = rows_call(hot[i], dx[i], n2[i], a_ff, lows, True, fac_d)
        g_a_ff.append(part)
        d_partial.append(tie(out, dh_load[0]) if i else out)
        out, part = rows_call(hot[i], y_slots[i], c_load[i], b_down, (0,), False, out)
        g_b_down.append(part)
        y_partial.append(out)

    def send_back(i, earlier):
        rows = scatter(d_partial[i])
        d_rows, ext = rows[:, :features].astype(F32), rows[:, features:]
        dw_own = ext[:, None, 4 * rank : 4 * rank + n_ffn].astype(F32)
        dw_top = jnp.sum(hits(rf_own[i], n_ffn) * dw_own, axis=2)
        d_logits = shares_back(wf_own[i], rf_own[i], n_ffn, dw_top)
        d_rows = d_rows + exact_mm(d_logits, router_ffn.astype(F32).T)
        dh1.append(c_own[i].astype(F32) + norm_back(h1[i], r2[i], gain_two, d_rows))
        dh_sent.append(tie(dh1[i], earlier).astype(BF16))
        dh_load.append(gather(dh_sent[i]))

    run_experts(0, 1, c_last)
    sum_rows(0)
    run_experts(1, 0, y_partial[0])
    send_back(0, dx[1][0])
    run_experts(1, 1, dh_sent[0])
    sum_rows(1)

    do, dwa, dq, dk, dv = ([None, None] for _ in range(5))
    g_a_o = jnp.zeros(a_o.shape, F32)
    g_b_o = jnp.zeros(b_o.shape, F32)
    for i in both:
        if i:
            send_back(1, dq[0])
        do[i], dwa[i], part_a, part_b = out_back_call(
            low1[i], sizes[i], dh_load[i], o[i], w_o, a_o, b_o
        )
        g_a_o, g_b_o = g_a_o + part_a, g_b_o + part_b
        if i:
            dq[1], dk[0], dv[0], dk[1], dv[1] = attend_cont_back(
                q[1], k[0], v[0], k[1], v[1], do[1], lse[1], dkp, dvp, cont_len
            )
        else:
            dq[0], dkp, dvp = attend_prompt_back(q[0], k[0], v[0], do[0], lse[0])
    y_own = scatter(tie(together(*y_partial), dh_load[1]))
    y_own = [y_own[span[0] : sum(span)] for span in spans]
    outs = [(h1[i] + y_own[i].astype(F32)).astype(BF16) for i in both]
    g_units, g_a_ff, g_b_down = sum(sums), sum(g_a_ff), sum(g_b_down)

    g_a_qkv = jnp.zeros((3 * rank, features), F32)
    g_b_qkv = jnp.zeros(b_qkv.shape, F32)
    grads, back = [], []
    earlier = ()
    dw_own = spread_blocks(together(*dwa).reshape(shards, -1, EXT))
    dw_own = sum(m[:, :tops].astype(F32) for m in dw_own)
    for i in both:
        rows, part_a, part_b = qkv_back_call(
            load,
            spans[i],
            dq[i],
            dk[i],
            dv[i],
            low1[i],
            w_query,
            w_kv,
            b_qkv,
            a_qkv[: 3 * rank],
            earlier,
        )
        earlier = (rows,)
        g_a_qkv, g_b_qkv = g_a_qkv + part_a, g_b_qkv + part_b
        back.append(rows)
    back = scatter(tie(together(*back), y_own[0]))
    for i in both:
        d_rows = back[spans[i][0] : sum(spans[i])].astype(F32)
        d_logits = shares_back(wa_own[i], ra_own[i], n_attn, dw_own[spans[i][0] : sum(spans[i])])
        d_rows = d_rows + exact_mm(d_logits, router_attn.astype(F32).T)
        grads.append(dh1[i] + norm_back(x_own[i].astype(F32), r1[i], gain_one, d_rows))
    adapters = ada_in.shape[0]
    pick_lines = jnp.broadcast_to(adapter_pick.astype(BF16)[:, None], (16, 128))

    partial = jnp.concatenate([g_a_qkv, g_a_ff, g_b_o, g_b_down], axis=0).astype(BF16)
    partial = partial.reshape(-1, shards, width).transpose(1, 0, 2)
    summed = sum(m.astype(F32) for m in spread_blocks(partial)).reshape(-1, rank, width)
    grads_own = [summed[:3], g_a_o[None], summed[3:5], g_b_qkv, summed[5:], g_units]
    lines = [g.astype(BF16).reshape(-1, 128) for g in grads_own]
    every = cube_gather(jnp.concatenate([pick_lines] + lines, axis=0), 0)
    picks = every[:, 0, 0].astype(F32)
    by_adapter = (picks[None, :] == jnp.arange(adapters, dtype=F32)[:, None]).astype(F32)
    total = jnp.sum(by_adapter[:, :, None, None] * every.astype(F32)[None], axis=1)
    out, start = [], pick_lines.shape[0]
    for line, grad in zip(lines, grads_own):
        out.append(total[:, start : start + line.shape[0]].reshape((adapters,) + grad.shape))
        start += line.shape[0]
    g_in = jnp.concatenate(out[:3], axis=1)
    g_out = jnp.concatenate(out[3:5], axis=1)

    shape_c = (1,) + cont_in.shape[1:]
    return (
        outs[0][None],
        outs[1].reshape(shape_c),
        grads[0][None],
        grads[1].reshape(shape_c),
        g_in,
        g_out,
        out[5][:, 2],
        out[5][:, :2],
    )


def solution(mesh):
    rows = (P("rep", "shard", None), P("rep", "shard", None, None))
    last = (
        P(None, None, None, "shard"),
        P(None, None, None, "shard"),
        P(None, None, "shard"),
        P(None, None, None, "shard"),
    )
    in_specs = (
        rows * 4
        + (P("rep"), P(), P(), P())
        + (P(None, None, "shard"),) * 3
        + (P(None, None, None, "shard"), P(None, "shard", None))
        + last
    )
    return jax.shard_map(
        on_device, mesh=mesh, in_specs=in_specs, out_specs=rows * 2 + last, check_vma=False
    )
```

profile of v0, /device:TPU:0, one launch (start us, length us, event | category | flops | bytes accessed | tf_op | source)
XLA Modules:
  0.0 1284.3 jit_solution(11509109598272662867)
XLA Ops:
  22.8 5.1 collective-permute-start
  28.9 8.1 collective-permute-done
  37.0 29.4 %collective-permute-done.1 = bf16[4,64,512]{2,1,0:T(8,128)(2,1)} collective-permute-done((bf16[4,64,512]{2,1,0:T(8,128)(2,1)S(1)}, bf16[4,64,512]{2,1,0:T(8,128)(2,1)}, u32[]{:S(2)}, u32[]{:S(2)}) %collective-permute-start.1) | collective-permute-done | bytes 262176 | tf_op jit(solution)/shard_map/ppermute | solution.py:785
  70.1 20.2 %collective-permute-done.3 = bf16[4,64,2048]{2,1,0:T(8,128)(2,1)} collective-permute-done((bf16[4,64,2048]{2,1,0:T(8,128)(2,1)S(1)}, bf16[4,64,2048]{2,1,0:T(8,128)(2,1)}, u32[]{:S(2)}, u32[]{:S(2)}) %collective-permute-start.3) | collective-permute-done | bytes 1048608 | tf_op jit(solution)/shard_map/ppermute | solution.py:800
  95.2 42.0 %collective-permute-done.4 = bf16[4,2,64,2048]{3,2,1,0:T(8,128)(2,1)} collective-permute-done((bf16[4,2,64,2048]{3,2,1,0:T(8,128)(2,1)}, bf16[4,2,64,2048]{3,2,1,0:T(8,128)(2,1)}, u32[]{:S(2)}, u32[]{:S(2)}) %collective-permute-start.4) | collective-permute-done | bytes 2097184 | tf_op jit(solution)/shard_map/ppermute | solution.py:800
  142.6 34.7 %all-gather.19.cloned.1.call-done = bf16[1920,2048]{1,0:T(8,128)(2,1)} async-done(((bf16[480,2048]{1,0:T(8,128)(2,1)}), bf16[1920,2048]{1,0:T(8,128)(2,1)}) %all-gather.19.cloned.1.call-update) | async-done | bytes 7864336 | tf_op jit(solution)/shard_map/all_gather | solution.py:771
  183.6 5.0 select_bitcast_fusion.1
  188.6 6.7 pad_maximum_fusion
  201.0 24.5 %qkv.2 = (bf16[2,1024,512]{2,1,0:T(8,128)(2,1)}, bf16[1024,512]{1,0:T(8,128)(2,1)}, bf16[1024,512]{1,0:T(8,128)(2,1)}, bf16[1024,128]{1,0:T(8,128)(2,1)}) custom-call(bf16[4,480,2048]{2,1,0:T(8,128)(2,1)} %bitcast.431, bf16[4,448,128]{2,1,0:T(8,128)(2,1)} %pad.9.routes, bf16[4,2048,512]{2,1,0:T(8,128)(2,1)} %refs_5_.3, bf16[2,2048,512]{2,1,0:T(8,128)(2,1)} %refs_6_.3, ...), custom_call_target="tpu_custom_call" | custom-call | flops 12884901888 | bytes 20447232 | tf_op jit(solution)/shard_map/qkv/pallas_call | solution.py:169
  227.9 13.5 %attend_prompt.1 = (bf16[2,1024,512]{2,1,0:T(8,128)(2,1)S(1)}, f32[4,2,1024,1]{3,2,1,0:T(8,128)}) custom-call(bf16[2,1024,512]{2,1,0:T(8,128)(2,1)} %get-tuple-element.63.q, bf16[1024,512]{1,0:T(8,128)(2,1)S(1)} %copy-done.4, bf16[1024,512]{1,0:T(8,128)(2,1)S(1)} %copy-done.7), custom_call_target="tpu_custom_call" | custom-call | flops 2147483648 | bytes 8388608 | tf_op jit(solution)/shard_map/attend_prompt/pallas_call | solution.py:703
  242.8 16.3 %project_out.2 = bf16[1024,2048]{1,0:T(8,128)(2,1)} custom-call(bf16[1024,128]{1,0:T(8,128)(2,1)} %get-tuple-element.62.ext.refs_4_, bf16[2,1024,512]{2,1,0:T(8,128)(2,1)} %copy-done.10, bf16[4,512,2048]{2,1,0:T(8,128)(2,1)} %bitcast.347, bf16[16,512]{1,0:T(8,128)(2,1)} %dynamic-slice_bitcast_fusion.10.fac_a, bf16[16,2048]{1,0:T(8,128)(2,1)} %bitcast.420), custom_call_target="tpu_custom_call" | custom-call | flops 8589934592 | bytes 14680064 | tf_op jit(solution)/shard_map/project_out/pallas_call | solution.py:217
  259.0 3.3 all-gather.11.cloned.1.call-done
  264.2 4.4 broadcast_add_fusion.earlier
  268.8 21.2 %qkv.3 = (bf16[2,768,512]{2,1,0:T(8,128)(2,1)}, bf16[768,512]{1,0:T(8,128)(2,1)}, bf16[768,512]{1,0:T(8,128)(2,1)}, bf16[768,128]{1,0:T(8,128)(2,1)}) custom-call(bf16[4,480,2048]{2,1,0:T(8,128)(2,1)} %bitcast.432, bf16[4,448,128]{2,1,0:T(8,128)(2,1)} %pad.9.routes, bf16[4,2048,512]{2,1,0:T(8,128)(2,1)} %refs_5_.3, bf16[2,2048,512]{2,1,0:T(8,128)(2,1)} %refs_6_.3, ...), custom_call_target="tpu_custom_call" | custom-call | flops 9663676416 | bytes 20447232 | tf_op jit(solution)/shard_map/qkv/pallas_call | solution.py:169
  292.3 26.7 %attend_cont.1 = (bf16[2,768,512]{2,1,0:T(8,128)(2,1)S(1)}, f32[4,2,768,1]{3,2,1,0:T(8,128)}) custom-call(bf16[2,768,512]{2,1,0:T(8,128)(2,1)} %get-tuple-element.68.q, bf16[1024,512]{1,0:T(8,128)(2,1)S(1)} %copy-done.5, bf16[1024,512]{1,0:T(8,128)(2,1)S(1)} %copy-done.8, bf16[768,512]{1,0:T(8,128)(2,1)S(1)} %copy-done.11, bf16[768,512]{1,0:T(8,128)(2,1)S(1)} %copy-done.13, ...), custom_call_target="tpu_custom_call" | custom-call | flops 3221225472 | bytes 6291456 | tf_op jit(solution)/shard_map/attend_cont/pallas_call | solution.py:710
  320.2 13.3 %project_out.3 = bf16[768,2048]{1,0:T(8,128)(2,1)} custom-call(bf16[768,128]{1,0:T(8,128)(2,1)} %get-tuple-element.67.ext.refs_4_, bf16[2,768,512]{2,1,0:T(8,128)(2,1)} %copy-done.3, bf16[4,512,2048]{2,1,0:T(8,128)(2,1)} %bitcast.348, bf16[16,512]{1,0:T(8,128)(2,1)} %dynamic-slice_bitcast_fusion.10.fac_a, bf16[16,2048]{1,0:T(8,128)(2,1)} %bitcast.421), custom_call_target="tpu_custom_call" | custom-call | flops 6442450944 | bytes 13107200 | tf_op jit(solution)/shard_map/project_out/pallas_call | solution.py:217
  335.3 8.8 reduce-scatter.7.cloned.1.call-done
  348.8 2.6 concatenate.151
  354.7 84.9 %all-gather.13.cloned.1.call-done.refs_1_.refs_2_ = bf16[4,256,2176]{2,1,0:T(8,128)(2,1)} async-done(((bf16[1,256,2176]{2,1,0:T(8,128)(2,1)}), bf16[4,256,2176]{2,1,0:T(8,128)(2,1)}) %all-gather.13.cloned.1.call-update) | async-done | bytes 4456464 | tf_op jit(solution)/shard_map/all_gather | solution.py:771
  441.4 3.8 broadcast_add_fusion.2.refs_7_
  451.5 3.4 subtract_convert_fusion.4
  455.3 7.8 concatenate.154.refs_2_
  463.1 62.2 %ffn.4 = (bf16[2,544,2176]{2,1,0:T(8,128)(2,1)}, bf16[2,544,2176]{2,1,0:T(8,128)(2,1)}, f32[3,16,1408]{2,1,0:T(8,128)}) custom-call(bf16[4,2,272,512]{3,2,1,0:T(8,128)(2,1)} %fusion.refs_0_.hot, bf16[4,256,2176]{2,1,0:T(8,128)(2,1)} %all-gather.13.cloned.1.call-done.refs_1_.refs_2_, bf16[4,256,2176]{2,1,0:T(8,128)(2,1)} %concatenate.154.refs_2_, ...), custom_call_target="tpu_custom_call" | custom-call | flops 37648072704 | bytes 52428800 | tf_op jit(solution)/shard_map/ffn/pallas_call | solution.py:489
  527.3 2.9 multiply_reduce_fusion.5
  539.0 77.2 %ffn.5 = (bf16[2,544,2176]{2,1,0:T(8,128)(2,1)}, bf16[2,544,2176]{2,1,0:T(8,128)(2,1)}, f32[3,16,1408]{2,1,0:T(8,128)}) custom-call(bf16[4,2,272,512]{3,2,1,0:T(8,128)(2,1)} %fusion.refs_0_.hot, bf16[4,256,2176]{2,1,0:T(8,128)(2,1)} %all-gather.13.cloned.1.call-done.refs_1_.refs_2_, bf16[4,256,2176]{2,1,0:T(8,128)(2,1)} %concatenate.154.refs_2_, ...), custom_call_target="tpu_custom_call" | custom-call | flops 37648072704 | bytes 52428800 | tf_op jit(solution)/shard_map/ffn/pallas_call | solution.py:489
  616.2 17.2 %slots_to_rows.4 = (bf16[1024,2176]{1,0:T(8,128)(2,1)}, f32[32,2048]{1,0:T(8,128)}) custom-call(bf16[4,2,272,512]{3,2,1,0:T(8,128)(2,1)} %fusion.refs_0_.hot, bf16[2,2,272,2176]{3,2,1,0:T(8,128)(2,1)} %bitcast.444, bf16[2,2,272,2176]{3,2,1,0:T(8,128)(2,1)} %bitcast.445, bf16[4,256,2176]{2,1,0:T(8,128)(2,1)} %all-gather.13.cloned.1.call-done.refs_1_.refs_2_, ...), custom_call_target="tpu_custom_call" | custom-call | flops 4848615424 | bytes 11698176 | tf_op jit(solution)/shard_map/slots_to_rows/pallas_call | solution.py:555
  635.6 18.6 %slots_to_rows.5 = (bf16[1024,2048]{1,0:T(8,128)(2,1)}, f32[16,2048]{1,0:T(8,128)}) custom-call(bf16[4,2,272,512]{3,2,1,0:T(8,128)(2,1)} %fusion.refs_0_.hot, bf16[2,2,272,2176]{3,2,1,0:T(8,128)(2,1)} %bitcast.351, bf16[2,2,272,2176]{3,2,1,0:T(8,128)(2,1)} %bitcast.352, bf16[4,256,2176]{2,1,0:T(8,128)(2,1)} %concatenate.154.refs_2_, ...), custom_call_target="tpu_custom_call" | custom-call | flops 4848615424 | bytes 11698176 | tf_op jit(solution)/shard_map/slots_to_rows/pallas_call | solution.py:555
  654.3 2.8 subtract_convert_fusion.5
  657.5 6.0 concatenate.170.refs_2_
  664.0 49.2 %ffn.6 = (bf16[2,416,2176]{2,1,0:T(8,128)(2,1)}, bf16[2,416,2176]{2,1,0:T(8,128)(2,1)}, f32[3,16,1408]{2,1,0:T(8,128)}) custom-call(bf16[4,2,208,384]{3,2,1,0:T(8,128)(2,1)} %fusion.5.refs_0_.hot, bf16[4,192,2176]{2,1,0:T(8,128)(2,1)} %all-gather.15.cloned.1.call-done.refs_1_.refs_2_, bf16[4,192,2176]{2,1,0:T(8,128)(2,1)} %concatenate.170.refs_2_, ...), custom_call_target="tpu_custom_call" | custom-call | flops 28789702656 | bytes 48234496 | tf_op jit(solution)/shard_map/ffn/pallas_call | solution.py:489
  715.0 31.1 %reduce-scatter.11.cloned.1.call-done = bf16[256,2176]{1,0:T(8,128)(2,1)} async-done(((bf16[1024,2176]{1,0:T(8,128)(2,1)}), bf16[256,2176]{1,0:T(8,128)(2,1)}) %reduce-scatter.11.cloned.1.call-update) | async-done | bytes 1114128 | tf_op jit(solution)/shard_map/reduce_scatter | solution.py:774
  747.2 3.2 multiply_reduce_fusion.1
  753.7 49.6 %ffn.7 = (bf16[2,416,2176]{2,1,0:T(8,128)(2,1)}, bf16[2,416,2176]{2,1,0:T(8,128)(2,1)}, f32[3,16,1408]{2,1,0:T(8,128)}) custom-call(bf16[4,2,208,384]{3,2,1,0:T(8,128)(2,1)} %fusion.5.refs_0_.hot, bf16[4,192,2176]{2,1,0:T(8,128)(2,1)} %all-gather.15.cloned.1.call-done.refs_1_.refs_2_, bf16[4,192,2176]{2,1,0:T(8,128)(2,1)} %concatenate.170.refs_2_, ...), custom_call_target="tpu_custom_call" | custom-call | flops 28789702656 | bytes 48234496 | tf_op jit(solution)/shard_map/ffn/pallas_call | solution.py:489
  803.3 10.5 slots_to_rows.6
  813.8 21.3 %all-gather.21.cloned.1.call-done = bf16[1024,2048]{1,0:T(8,128)(2,1)} async-done(((bf16[256,2048]{1,0:T(8,128)(2,1)}), bf16[1024,2048]{1,0:T(8,128)(2,1)}) %all-gather.21.cloned.1.call-update) | async-done | bytes 4194320 | tf_op jit(solution)/shard_map/all_gather | solution.py:771
  836.9 3.9 broadcast_add_fusion.1
  841.0 20.3 %project_out_back.2 = (bf16[2,1024,512]{2,1,0:T(8,128)(2,1)}, bf16[1024,128]{1,0:T(8,128)(2,1)}, f32[16,512]{1,0:T(8,128)}, f32[16,2048]{1,0:T(8,128)}) custom-call(bf16[1024,128]{1,0:T(8,128)(2,1)} %get-tuple-element.62.ext.refs_4_, bf16[4,256,2048]{2,1,0:T(8,128)(2,1)} %bitcast.441, bf16[2,1024,512]{2,1,0:T(8,128)(2,1)} %copy-done.10, ...), custom_call_target="tpu_custom_call" | custom-call | flops 8589934592 | bytes 16777216 | tf_op jit(solution)/shard_map/project_out_back/pallas_call | solution.py:277
  861.3 23.8 %attend_prompt_back.1 = (bf16[2,1024,512]{2,1,0:T(8,128)(2,1)S(1)}, f32[1024,512]{1,0:T(8,128)}, f32[1024,512]{1,0:T(8,128)}) custom-call(bf16[2,1024,512]{2,1,0:T(8,128)(2,1)} %get-tuple-element.63.q, bf16[1024,512]{1,0:T(8,128)(2,1)S(1)} %copy-done.6, bf16[1024,512]{1,0:T(8,128)(2,1)S(1)} %copy-done.9, bf16[2,1024,512]{2,1,0:T(8,128)(2,1)} %get-tuple-element.84.do, ...), custom_call_target="tpu_custom_call" | custom-call | flops 6442450944 | bytes 8388608 | tf_op jit(solution)/shard_map/attend_prompt_back/pallas_call | solution.py:717
  886.3 16.6 %reduce-scatter.13.cloned.1.call-done = bf16[192,2176]{1,0:T(8,128)(2,1)} async-done(((bf16[768,2176]{1,0:T(8,128)(2,1)}), bf16[192,2176]{1,0:T(8,128)(2,1)}) %reduce-scatter.13.cloned.1.call-update) | async-done | bytes 835600 | tf_op jit(solution)/shard_map/reduce_scatter | solution.py:774
  904.0 3.2 multiply_reduce_fusion.4
  910.0 10.0 slots_to_rows.7
  920.0 53.7 %all-gather.23.cloned.1.call-done = bf16[768,2048]{1,0:T(8,128)(2,1)} async-done(((bf16[192,2048]{1,0:T(8,128)(2,1)}), bf16[768,2048]{1,0:T(8,128)(2,1)}) %all-gather.23.cloned.1.call-update) | async-done | bytes 3145744 | tf_op jit(solution)/shard_map/all_gather | solution.py:771
  975.6 8.9 maximum_add_fusion
  984.6 16.8 %project_out_back.3 = (bf16[2,768,512]{2,1,0:T(8,128)(2,1)}, bf16[768,128]{1,0:T(8,128)(2,1)}, f32[16,512]{1,0:T(8,128)}, f32[16,2048]{1,0:T(8,128)}) custom-call(bf16[768,128]{1,0:T(8,128)(2,1)} %get-tuple-element.67.ext.refs_4_, bf16[4,192,2048]{2,1,0:T(8,128)(2,1)} %bitcast.443, bf16[2,768,512]{2,1,0:T(8,128)(2,1)} %copy-done.3, ...), custom_call_target="tpu_custom_call" | custom-call | flops 6442450944 | bytes 14680064 | tf_op jit(solution)/shard_map/project_out_back/pallas_call | solution.py:277
  1001.4 33.0 %attend_cont_back.1 = (bf16[2,768,512]{2,1,0:T(8,128)(2,1)}, bf16[1024,512]{1,0:T(8,128)(2,1)S(1)}, bf16[1024,512]{1,0:T(8,128)(2,1)S(1)}, bf16[768,512]{1,0:T(8,128)(2,1)S(1)}, bf16[768,512]{1,0:T(8,128)(2,1)S(1)}) custom-call(bf16[2,768,512]{2,1,0:T(8,128)(2,1)} %get-tuple-element.68.q, bf16[1024,512]{1,0:T(8,128)(2,1)} %get-tuple-element.64.k.kp, ...), custom_call_target="tpu_custom_call" | custom-call | flops 9663676416 | bytes 6291456 | tf_op jit(solution)/shard_map/attend_cont_back/pallas_call | solution.py:724
  1038.1 25.8 %qkv_back.2 = (bf16[1024,2048]{1,0:T(8,128)(2,1)}, f32[48,2048]{1,0:T(8,128)}, f32[3,16,512]{2,1,0:T(8,128)}) custom-call(bf16[4,480,2048]{2,1,0:T(8,128)(2,1)} %bitcast.433, bf16[2,1024,512]{2,1,0:T(8,128)(2,1)} %copy-done.2, bf16[1024,512]{1,0:T(8,128)(2,1)} %copy-done.17, bf16[1024,512]{1,0:T(8,128)(2,1)} %copy-done.18, ...), custom_call_target="tpu_custom_call" | custom-call | flops 12884901888 | bytes 28311552 | tf_op jit(solution)/shard_map/qkv_back/pallas_call | solution.py:348
  1063.8 21.1 %qkv_back.3 = (bf16[768,2048]{1,0:T(8,128)(2,1)}, f32[48,2048]{1,0:T(8,128)}, f32[3,16,512]{2,1,0:T(8,128)}) custom-call(bf16[4,480,2048]{2,1,0:T(8,128)(2,1)} %bitcast.434, bf16[2,768,512]{2,1,0:T(8,128)(2,1)} %get-tuple-element.94.refs_1_, bf16[768,512]{1,0:T(8,128)(2,1)} %copy-done.15, bf16[768,512]{1,0:T(8,128)(2,1)} %copy-done.16, ...), custom_call_target="tpu_custom_call" | custom-call | flops 9663676416 | bytes 28311552 | tf_op jit(solution)/shard_map/qkv_back/pallas_call | solution.py:348
  1085.0 26.0 %reduce-scatter.15.cloned.1.call-done = bf16[448,2048]{1,0:T(8,128)(2,1)} async-done(((bf16[1792,2048]{1,0:T(8,128)(2,1)}), bf16[448,2048]{1,0:T(8,128)(2,1)}) %reduce-scatter.15.cloned.1.call-update) | async-done | bytes 1835024 | tf_op jit(solution)/shard_map/reduce_scatter | solution.py:774
  1112.9 8.9 maximum_add_fusion.1
  1127.9 3.0 collective-permute-start.10
  1133.7 12.5 collective-permute-done.10
  1153.5 7.1 collective-permute-done.12
  1164.3 9.8 collective-permute-start.6
  1177.3 3.5 collective-permute-done.6
  1180.8 5.6 collective-permute-done.7
  1186.4 4.9 collective-permute-done.8
  1193.2 10.1 multiply_reduce_fusion
  1212.8 2.9 reshape.665
  1215.7 2.6 slice.321
  1222.8 43.3 %reduce-scatter.17.cloned.1.call-done = bf16[448,2048]{1,0:T(8,128)(2,1)} async-done(((bf16[1792,2048]{1,0:T(8,128)(2,1)}), bf16[448,2048]{1,0:T(8,128)(2,1)}) %reduce-scatter.17.cloned.1.call-update) | async-done | bytes 1835024 | tf_op jit(solution)/shard_map/reduce_scatter | solution.py:774
  1266.1 2.8 multiply_reduce_fusion.3
  1269.0 2.8 fusion.13
  1272.0 2.5 subtract_add_fusion
  1274.5 3.0 fusion.12
  (475 shorter events, 133.6 us)
Async XLA Ops:
  7.2 438.1 %copy-start = (bf16[8,16,1408]{2,1,0:T(8,128)(2,1)S(1)}, bf16[8,16,1408]{2,1,0:T(8,128)(2,1)}, u32[]{:S(2)}) copy-start(bf16[8,16,1408]{2,1,0:T(8,128)(2,1)} %param.40) | copy-start | bytes 1081348
  7.2 8.5 copy-start.19
  7.2 8.1 copy-start.21
  7.2 170.1 %all-gather.19.cloned.1.call-start = ((), (), s32[]{:S(2)}) async-start(), calls=%async_computation.16 | async-start | bytes 9830400 | tf_op jit(solution)/shard_map/all_gather | solution.py:771
  8.1 7.8 copy-start.66
  10.3 5.7 copy-start.88
  19.4 242.9 %all-gather.11.cloned.1.call-start = ((), (), s32[]{:S(2)}) async-start(), calls=%async_computation.6 | async-start | bytes 5242880 | tf_op jit(solution)/shard_map/all_gather | solution.py:771
  22.8 14.2 %collective-permute-start = (bf16[4,64,512]{2,1,0:T(8,128)(2,1)S(1)}, bf16[4,64,512]{2,1,0:T(8,128)(2,1)}, u32[]{:S(2)}, u32[]{:S(2)}) collective-permute-start(bf16[4,64,512]{2,1,0:T(8,128)(2,1)S(1)} %get-tuple-element.158), channel_id=1, source_target_pairs={{0,3},{1,0},{2,1},{3,2},{4,7},{5,4},{6,5},{7,6},{8,11},{9,8},{10,9... | collective-permute-start | bytes 786440 | tf_op jit(solution)/shard_map/ppermute | solution.py:785
  27.9 38.6 %collective-permute-start.1 = (bf16[4,64,512]{2,1,0:T(8,128)(2,1)S(1)}, bf16[4,64,512]{2,1,0:T(8,128)(2,1)}, u32[]{:S(2)}, u32[]{:S(2)}) collective-permute-start(bf16[4,64,512]{2,1,0:T(8,128)(2,1)S(1)} %get-tuple-element.157), channel_id=1, source_target_pairs={{0,2},{1,3},{2,0},{3,1},{4,6},{5,7},{6,4},{7,5},{8,10},{9,11},{10,... | collective-permute-start | bytes 786440 | tf_op jit(solution)/shard_map/ppermute | solution.py:785
  27.9 38.6 %collective-permute-start.2 = (bf16[4,64,512]{2,1,0:T(8,128)(2,1)S(1)}, bf16[4,64,512]{2,1,0:T(8,128)(2,1)}, u32[]{:S(2)}, u32[]{:S(2)}) collective-permute-start(bf16[4,64,512]{2,1,0:T(8,128)(2,1)S(1)} %get-tuple-element.156), channel_id=1, source_target_pairs={{0,1},{1,2},{2,3},{3,0},{4,5},{5,6},{6,7},{7,4},{8,9},{9,10},{10,1... | collective-permute-start | bytes 786440 | tf_op jit(solution)/shard_map/ppermute | solution.py:785
  68.5 21.8 %collective-permute-start.3 = (bf16[4,64,2048]{2,1,0:T(8,128)(2,1)S(1)}, bf16[4,64,2048]{2,1,0:T(8,128)(2,1)}, u32[]{:S(2)}, u32[]{:S(2)}) collective-permute-start(bf16[4,64,2048]{2,1,0:T(8,128)(2,1)S(1)} %pad_maximum_fusion.8), channel_id=1, source_target_pairs={{0,16},{4,20},{8,24},{12,28},{16,0},{20,4},{24,8},{28,12},{1,17},{... | collective-permute-start | bytes 3145736 | tf_op jit(solution)/shard_map/ppermute | solution.py:800
  93.7 43.5 %collective-permute-start.4 = (bf16[4,2,64,2048]{3,2,1,0:T(8,128)(2,1)}, bf16[4,2,64,2048]{3,2,1,0:T(8,128)(2,1)}, u32[]{:S(2)}, u32[]{:S(2)}) collective-permute-start(bf16[4,2,64,2048]{3,2,1,0:T(8,128)(2,1)} %pad_maximum_fusion.3), channel_id=1, source_target_pairs={{0,8},{4,12},{8,0},{12,4},{16,24},{20,28},{24,16},{28,20},{1,9},{5... | collective-permute-start | bytes 6291464 | tf_op jit(solution)/shard_map/ppermute | solution.py:800
  139.4 39.8 %copy-start.39 = (bf16[1,256,2048]{2,1,0:T(8,128)(2,1)S(1)}, bf16[1,256,2048]{2,1,0:T(8,128)(2,1)}, u32[]{:S(2)}) copy-start(bf16[1,256,2048]{2,1,0:T(8,128)(2,1)} %param.23) | copy-start | bytes 3145732
  142.6 41.0 %collective-permute-start.5 = (bf16[4,2,2,64,2048]{4,3,2,1,0:T(8,128)(2,1)}, bf16[4,2,2,64,2048]{4,3,2,1,0:T(8,128)(2,1)}, u32[]{:S(2)}, u32[]{:S(2)}) collective-permute-start(bf16[4,2,2,64,2048]{4,3,2,1,0:T(8,128)(2,1)} %pad_maximum_fusion.1), channel_id=1, source_target_pairs={{0,4},{4,0},{8,12},{12,8},{16,20},{20,16},{24,28},{28,24},{1,5},{5... | collective-permute-start | bytes 12582920 | tf_op jit(solution)/shard_map/ppermute | solution.py:800
  180.2 163.8 %reduce-scatter.7.cloned.1.call-start = ((), (), s32[]{:S(2)}) async-start(), calls=%async_computation.7 | async-start | bytes 5242880 | tf_op jit(solution)/shard_map/reduce_scatter | solution.py:774
  197.1 28.3 %copy-start.56 = (bf16[6,8,4,512]{3,1,2,0:T(8,128)(2,1)}, bf16[6,8,4,512]{3,1,2,0:T(8,128)(2,1)S(1)}, u32[]{:S(2)}) copy-start(bf16[6,8,4,512]{3,1,2,0:T(8,128)(2,1)S(1)} %copy.333) | copy-start | bytes 589828
  268.6 170.9 %all-gather.13.cloned.1.call-start = ((), (), s32[]{:S(2)}) async-start(), calls=%async_computation.8 | async-start | bytes 5570560 | tf_op jit(solution)/shard_map/all_gather | solution.py:771
  268.8 266.4 %copy-start.51 = (bf16[4,8,4,512]{3,1,2,0:T(8,128)(2,1)}, bf16[4,8,4,512]{3,1,2,0:T(8,128)(2,1)S(1)}, u32[]{:S(2)}) copy-start(bf16[4,8,4,512]{3,1,2,0:T(8,128)(2,1)S(1)} %copy.335) | copy-start | bytes 393220
  268.8 21.2 %copy-start.5 = (bf16[1024,512]{1,0:T(8,128)(2,1)S(1)}, bf16[1024,512]{1,0:T(8,128)(2,1)}, u32[]{:S(2)}) copy-start(bf16[1024,512]{1,0:T(8,128)(2,1)} %get-tuple-element.64.k.kp) | copy-start | bytes 3145732
  268.8 21.2 %copy-start.8 = (bf16[1024,512]{1,0:T(8,128)(2,1)S(1)}, bf16[1024,512]{1,0:T(8,128)(2,1)}, u32[]{:S(2)}) copy-start(bf16[1024,512]{1,0:T(8,128)(2,1)} %get-tuple-element.65.v.vp) | copy-start | bytes 3145732
  347.9 5.9 copy-start.75
  353.8 173.5 %reduce-scatter.9.cloned.1.call-start = ((), (), s32[]{:S(2)}) async-start(), calls=%async_computation.9 | async-start | bytes 3932160 | tf_op jit(solution)/shard_map/reduce_scatter | solution.py:774
  445.2 209.0 %all-gather.17.cloned.1.call-start = ((), (), s32[]{:S(2)}) async-start(), calls=%async_computation.11 | async-start | bytes 3932160 | tf_op jit(solution)/shard_map/all_gather | solution.py:771
  449.1 5.8 copy-start.54
  525.4 5.5 copy-start.22
  527.3 6.0 copy-start.45
  530.9 376.3 %copy-start.81 = (f32[192]{0:T(256)}, f32[192]{0:T(256)S(1)}, u32[]{:S(2)}) copy-start(f32[192]{0:T(256)S(1)} %get-tuple-element.185) | copy-start | bytes 2308
  534.4 129.6 %all-gather.15.cloned.1.call-start = ((), (), s32[]{:S(2)}) async-start(), calls=%async_computation.10 | async-start | bytes 4177920 | tf_op jit(solution)/shard_map/all_gather | solution.py:771
  538.9 207.1 %reduce-scatter.11.cloned.1.call-start = ((), (), s32[]{:S(2)}) async-start(), calls=%async_computation.12 | async-start | bytes 5570560 | tf_op jit(solution)/shard_map/reduce_scatter | solution.py:774
  633.4 201.7 %all-gather.21.cloned.1.call-start = ((), (), s32[]{:S(2)}) async-start(), calls=%async_computation.17 | async-start | bytes 5242880 | tf_op jit(solution)/shard_map/all_gather | solution.py:771
  635.6 18.6 %copy-start.55 = (bf16[2,8,4,512]{3,1,2,0:T(8,128)(2,1)S(1)}, bf16[2,8,4,512]{3,1,2,0:T(8,128)(2,1)}, u32[]{:S(2)}) copy-start(bf16[2,8,4,512]{3,1,2,0:T(8,128)(2,1)} %copy-done.54) | copy-start | bytes 196612
  664.0 83.1 %copy-start.72 = (s32[1,256,2]{1,2,0:T(2,128)S(1)}, s32[1,256,2]{1,2,0:T(2,128)}, u32[]{:S(2)}) copy-start(s32[1,256,2]{1,2,0:T(2,128)} %param.27) | copy-start | bytes 6148
  664.0 83.1 %copy-start.76 = (f32[256]{0:T(256)S(1)}, f32[256]{0:T(256)}, u32[]{:S(2)}) copy-start(f32[256]{0:T(256)} %copy-done.75) | copy-start | bytes 3076
  664.0 83.1 %copy-start.84 = (f32[256]{0:T(256)S(1)}, f32[256]{0:T(256)}, u32[]{:S(2)}) copy-start(f32[256]{0:T(256)} %copy-done.83) | copy-start | bytes 3076
  747.2 4.6 copy-start.25
  747.2 4.6 copy-start.40
  753.6 149.2 %reduce-scatter.13.cloned.1.call-start = ((), (), s32[]{:S(2)}) async-start(), calls=%async_computation.13 | async-start | bytes 4177920 | tf_op jit(solution)/shard_map/reduce_scatter | solution.py:774
  840.9 20.4 %copy-start.6 = (bf16[1024,512]{1,0:T(8,128)(2,1)S(1)}, bf16[1024,512]{1,0:T(8,128)(2,1)}, u32[]{:S(2)}) copy-start(bf16[1024,512]{1,0:T(8,128)(2,1)} %get-tuple-element.64.k.kp) | copy-start | bytes 3145732
  840.9 132.8 %all-gather.23.cloned.1.call-start = ((), (), s32[]{:S(2)}) async-start(), calls=%async_computation.18 | async-start | bytes 3932160 | tf_op jit(solution)/shard_map/all_gather | solution.py:771
  840.9 20.3 %copy-start.9 = (bf16[1024,512]{1,0:T(8,128)(2,1)S(1)}, bf16[1024,512]{1,0:T(8,128)(2,1)}, u32[]{:S(2)}) copy-start(bf16[1024,512]{1,0:T(8,128)(2,1)} %get-tuple-element.65.v.vp) | copy-start | bytes 3145732
  885.1 22.1 %copy-start.2 = (bf16[2,1024,512]{2,1,0:T(8,128)(2,1)}, bf16[2,1024,512]{2,1,0:T(8,128)(2,1)S(1)}, u32[]{:S(2)}) copy-start(bf16[2,1024,512]{2,1,0:T(8,128)(2,1)S(1)} %get-tuple-element.86.refs_1_) | copy-start | bytes 6291460
  909.9 201.1 %reduce-scatter.15.cloned.1.call-start = ((), (), s32[]{:S(2)}) async-start(), calls=%async_computation.14 | async-start | bytes 9175040 | tf_op jit(solution)/shard_map/reduce_scatter | solution.py:774
  984.5 16.9 %copy-start.12 = (bf16[768,512]{1,0:T(8,128)(2,1)S(1)}, bf16[768,512]{1,0:T(8,128)(2,1)}, u32[]{:S(2)}) copy-start(bf16[768,512]{1,0:T(8,128)(2,1)} %get-tuple-element.69.k) | copy-start | bytes 2359300
  984.5 16.9 %copy-start.14 = (bf16[768,512]{1,0:T(8,128)(2,1)S(1)}, bf16[768,512]{1,0:T(8,128)(2,1)}, u32[]{:S(2)}) copy-start(bf16[768,512]{1,0:T(8,128)(2,1)} %get-tuple-element.70.v) | copy-start | bytes 2359300
  984.5 281.6 %reduce-scatter.17.cloned.1.call-start = ((), (), s32[]{:S(2)}) async-start(), calls=%async_computation.15 | async-start | bytes 9175040 | tf_op jit(solution)/shard_map/reduce_scatter | solution.py:774
  1121.9 5.7 copy-start.59
  1121.9 5.7 copy-start.60
  1127.7 25.4 %copy-start.74 = (s32[192,2]{0,1:T(2,128)S(1)}, s32[192,2]{0,1:T(2,128)}, u32[]{:S(2)}) copy-start(s32[192,2]{0,1:T(2,128)} %copy-done.73) | copy-start | bytes 4612
  1127.7 25.4 %copy-start.44 = (bf16[256,2048]{1,0:T(8,128)(2,1)S(1)}, bf16[256,2048]{1,0:T(8,128)(2,1)}, u32[]{:S(2)}) copy-start(bf16[256,2048]{1,0:T(8,128)(2,1)} %copy-done.43) | copy-start | bytes 3145732
  1127.9 18.3 %collective-permute-start.10 = (bf16[112,512]{1,0:T(8,128)(2,1)S(1)}, bf16[112,512]{1,0:T(8,128)(2,1)S(1)}, u32[]{:S(2)}, u32[]{:S(2)}) collective-permute-start(bf16[112,512]{1,0:T(8,128)(2,1)S(1)} %get-tuple-element.165), channel_id=1, source_target_pairs={{0,2},{1,3},{2,0},{3,1},{4,6},{5,7},{6,4},{7,5},{8,10},{9,11},{10,... | collective-permute-start | bytes 344072 | tf_op jit(solution)/shard_map/ppermute | solution.py:785
  1130.9 16.7 %collective-permute-start.11 = (bf16[112,512]{1,0:T(8,128)(2,1)S(1)}, bf16[112,512]{1,0:T(8,128)(2,1)S(1)}, u32[]{:S(2)}, u32[]{:S(2)}) collective-permute-start(bf16[112,512]{1,0:T(8,128)(2,1)S(1)} %get-tuple-element.164), channel_id=1, source_target_pairs={{0,3},{1,0},{2,1},{3,2},{4,7},{5,4},{6,5},{7,6},{8,11},{9,8},{10,9... | collective-permute-start | bytes 344072 | tf_op jit(solution)/shard_map/ppermute | solution.py:785
  1131.8 15.8 %collective-permute-start.9 = (bf16[112,512]{1,0:T(8,128)(2,1)S(1)}, bf16[112,512]{1,0:T(8,128)(2,1)S(1)}, u32[]{:S(2)}, u32[]{:S(2)}) collective-permute-start(bf16[112,512]{1,0:T(8,128)(2,1)S(1)} %get-tuple-element.163), channel_id=1, source_target_pairs={{0,1},{1,2},{2,3},{3,0},{4,5},{5,6},{6,7},{7,4},{8,9},{9,10},{10,1... | collective-permute-start | bytes 344072 | tf_op jit(solution)/shard_map/ppermute | solution.py:785
  1148.4 14.7 %copy-start.77 = (s32[1,256,2]{1,2,0:T(2,128)S(1)}, s32[1,256,2]{1,2,0:T(2,128)}, u32[]{:S(2)}) copy-start(s32[1,256,2]{1,2,0:T(2,128)} %param.25) | copy-start | bytes 6148
  1148.4 14.8 %copy-start.86 = (f32[192]{0:T(256)S(1)}, f32[192]{0:T(256)}, u32[]{:S(2)}) copy-start(f32[192]{0:T(256)} %copy-done.85) | copy-start | bytes 2308
  1148.4 14.8 %copy-start.64 = (bf16[1024,128]{1,0:T(8,128)(2,1)S(1)}, bf16[1024,128]{1,0:T(8,128)(2,1)}, u32[]{:S(2)}) copy-start(bf16[1024,128]{1,0:T(8,128)(2,1)} %get-tuple-element.98) | copy-start | bytes 786436
  1151.6 9.0 collective-permute-start.12
  1161.6 15.4 %collective-permute-start.13 = (bf16[2,1248,128]{2,1,0:T(8,128)(2,1)S(1)}, bf16[2,1248,128]{2,1,0:T(8,128)(2,1)S(1)}, u32[]{:S(2)}, u32[]{:S(2)}) collective-permute-start(bf16[2,1248,128]{2,1,0:T(8,128)(2,1)S(1)} %pad_maximum_fusion.10), channel_id=1, source_target_pairs={{0,8},{4,12},{8,0},{12,4},{16,24},{20,28},{24,16},{28,20},{1,9},{5... | collective-permute-start | bytes 1916936 | tf_op jit(solution)/shard_map/ppermute | solution.py:800
  1164.3 16.5 %collective-permute-start.6 = (bf16[448,128]{0,1:T(8,128)(2,1)S(1)}, bf16[448,128]{0,1:T(8,128)(2,1)}, u32[]{:S(2)}, u32[]{:S(2)}) collective-permute-start(bf16[448,128]{0,1:T(8,128)(2,1)S(1)} %copy.285), channel_id=1, source_target_pairs={{0,1},{1,2},{2,3},{3,0},{4,5},{5,6},{6,7},{7,4},{8,9},{9,10},{10,1... | collective-permute-start | bytes 344072 | tf_op jit(solution)/shard_map/ppermute | solution.py:785
  1174.2 12.1 collective-permute-start.7
  1174.4 16.8 %collective-permute-start.8 = (bf16[448,128]{0,1:T(8,128)(2,1)S(1)}, bf16[448,128]{0,1:T(8,128)(2,1)S(1)}, u32[]{:S(2)}, u32[]{:S(2)}) collective-permute-start(bf16[448,128]{0,1:T(8,128)(2,1)S(1)} %copy.287), channel_id=1, source_target_pairs={{0,3},{1,0},{2,1},{3,2},{4,7},{5,4},{6,5},{7,6},{8,11},{9,8},{10,9... | collective-permute-start | bytes 344072 | tf_op jit(solution)/shard_map/ppermute | solution.py:785
  1177.2 14.9 %collective-permute-start.14 = (bf16[2,2,1248,128]{3,2,1,0:T(8,128)(2,1)S(1)}, bf16[2,2,1248,128]{3,2,1,0:T(8,128)(2,1)S(1)}, u32[]{:S(2)}, u32[]{:S(2)}) collective-permute-start(bf16[2,2,1248,128]{3,2,1,0:T(8,128)(2,1)S(1)} %pad_maximum_fusion.7), channel_id=1, source_target_pairs={{0,4},{4,0},{8,12},{12,8},{16,20},{20,16},{24,28},{28,24},{1,5},{5... | collective-permute-start | bytes 3833864 | tf_op jit(solution)/shard_map/ppermute | solution.py:800
  1219.5 46.6 %copy-start.67 = (f32[1,2048]{1,0:T(1,128)S(1)}, f32[1,2048]{1,0:T(1,128)}, u32[]{:S(2)}) copy-start(f32[1,2048]{1,0:T(1,128)} %copy-done.66) | copy-start | bytes 24580
  1222.8 46.1 %copy-start.20 = (bf16[1,256,2048]{2,1,0:T(8,128)(2,1)S(1)}, bf16[1,256,2048]{2,1,0:T(8,128)(2,1)}, u32[]{:S(2)}) copy-start(bf16[1,256,2048]{2,1,0:T(8,128)(2,1)} %param.21) | copy-start | bytes 3145732
  1266.1 5.8 copy-start.53
  (64 other events, 147.8 us)
Sparse Core Ops, SparseCore 0:
  19.6 157.7 all-gather.18
  180.4 81.9 all-gather.10
  268.8 75.2 reduce-scatter.6
  353.9 85.5 all-gather.12
  445.3 58.7 reduce-scatter.8
  534.5 62.3 all-gather.16
  598.6 65.3 all-gather.14
  666.4 79.6 reduce-scatter.10
  753.8 81.2 all-gather.20
  841.0 61.8 reduce-scatter.12
  910.0 63.6 all-gather.22
  984.6 126.3 reduce-scatter.14
  1122.0 144.0 reduce-scatter.16
where the time goes:
time: 1290 us; the launch traced here: 1280 us
  Pallas kernels  551 us (43%)
  waiting for transfers between devices  459 us (36%)
  other arithmetic  110 us (9%)
  local copies, waits for them, and re-layouts  88.3 us (7%)
  starting transfers between devices  30.7 us (2%)
  between operations  24.6 us (2%)
  matrix products  20.7 us (2%)
    pallas_call x4, Pallas kernels, ffn_call(): pl.pallas_call(kernel, grid=(experts,), in_specs=[pl.BlockSpec((1,) + hot...  238 us
    all_gather x7, waiting for transfers between devices, gather(): return lax.all_gather(values, 'shard', axis=0)  198 us
    reduce_scatter x6, waiting for transfers between devices, scatter(): return lax.psum_scatter(values, 'shard', scatter_dimension=0, tiled=True)  126 us
    ppermute x6, waiting for transfers between devices, cube_gather(): other = lax.ppermute(values, 'rep', [(k, k ^ bit) for k in range(reps)])  69.4 us
    ppermute x9, waiting for transfers between devices, spread_blocks(): out.append(lax.ppermute(block(shard_id + hop), 'shard', pairs))  65.4 us
    pallas_call x4, Pallas kernels, rows_call(): pl.pallas_call(kernel, grid=(pairs,), in_specs=[by_pair(experts, slots, r...  56.3 us
    pallas_call x2, Pallas kernels, qkv_back_call(): pl.pallas_call(kernel, grid=(total // (2 * rows),), in_specs=[pl.BlockSpe...  46.9 us
    pallas_call x2, Pallas kernels, qkv_call(): pl.pallas_call(functools.partial(qkv_kernel, span, tops, rank), grid=(sha...  45.7 us
  transfers between devices with their start and end apart: 28, of which 21 were waited for; matrix products, arithmetic and copies ran while one was open for 9% of the time, Pallas kernels for 43%

commit v1 on v0

--- a/solution.py
+++ b/solution.py
@@ -526,17 +526,18 @@
 
 def rows_call(hot, parts, source, fac, lows, keep, earlier):
     experts, pairs, slots, rows = hot.shape
-    count, _, wide = parts[0].shape
+    wide = parts[0].shape[2]
     rank = fac.shape[0] // len(lows)
     features = wide - EXT
-    parts = [m.reshape(count, pairs, slots, wide) for m in parts]
+    parts = [m.reshape(-1, pairs, slots, wide) for m in parts]
     by_pair = lambda n, *s: pl.BlockSpec((n, 1) + s, lambda p: (0, p, 0, 0))
 
     def kernel(hot, *refs):
         values, source, fac, _, out, grad = refs[: len(parts)], *refs[len(parts) :]
         total = None
+        slots_of = [ref[n, 0] for ref in values for n in range(ref.shape[0])]
         for e in range(experts):
-            here = dot_tn(hot[e, 0], values[e // count][e % count, 0])
+            here = dot_tn(hot[e, 0], slots_of[e])
             total = here if total is None else total + here
         low = [total[:, features + at : features + at + rank] for at in lows]
         low = split_low(jnp.concatenate(low, axis=1))
@@ -556,7 +557,7 @@
         kernel,
         grid=(pairs,),
         in_specs=[by_pair(experts, slots, rows)]
-        + [by_pair(count, slots, wide) for _ in parts]
+        + [by_pair(m.shape[0], slots, wide) for m in parts]
         + [
             pl.BlockSpec((2,) + source.shape[1:], lambda p: (p, 0, 0)),
             whole(*fac.shape),
@@ -867,9 +868,10 @@
     fac_gu = jnp.stack([jnp.concatenate(m + [blank] * (EXT // (2 * rank) - 2), axis=0) for m in fac_gu])
     fac_d = jnp.concatenate([twice(own_down)] + [blank] * (EXT // (2 * rank) - 1), axis=0).T
     half = n_ffn // 2
+    ahead = max(1, half // 2)
     y_slots, dx, sums = [[], []], [[], []], []
 
-    def run_experts(i, part, earlier):
+    def run_experts(i, begin, count, earlier):
         one, two, three = ffn_call(
             hot[i],
             n2[i],
@@ -880,8 +882,8 @@
             fac_d,
             rank,
             earlier,
-            part * half,
-            half,
+            begin,
+            count,
         )
         y_slots[i].append(one)
         dx[i].append(two)
@@ -896,7 +898,7 @@
         if i:
             partial[1] = tie(partial[1], n2[0])
             c_load[0] = beside_low(c_load[0])
-            run_experts(0, 0, partial[1])
+            run_experts(0, 0, ahead, partial[1])
         hidden = x_own[i].astype(F32) + scatter(partial[i]).astype(F32)
         normed, inverse = norm_rows(hidden, gain_two)
         normed = normed.astype(BF16)
@@ -937,11 +939,11 @@
         dh_sent.append(tie(dh1[i], earlier).astype(BF16))
         dh_load.append(gather(dh_sent[i]))
 
-    run_experts(0, 1, c_last)
+    run_experts(0, ahead, n_ffn - ahead, c_last)
     sum_rows(0)
-    run_experts(1, 0, y_partial[0])
+    run_experts(1, 0, half, y_partial[0])
     send_back(0, dx[1][0])
-    run_experts(1, 1, dh_sent[0])
+    run_experts(1, half, n_ffn - half, dh_sent[0])
     sum_rows(1)
 
     do, dwa, dq, dk, dv = ([None, None] for _ in range(5))
@@ -969,8 +971,8 @@
     g_b_qkv = jnp.zeros(b_qkv.shape, F32)
     grads, back = [], []
     earlier = ()
-    dw_own = spread_blocks(together(*dwa).reshape(shards, -1, EXT))
-    dw_own = sum(m[:, :tops].astype(F32) for m in dw_own)
+    dw_own = together(*(m[:, :tops] for m in dwa)).reshape(shards, -1, tops).transpose(0, 2, 1)
+    dw_own = sum(m.astype(F32) for m in spread_blocks(dw_own)).T
     for i in both:
         rows, part_a, part_b = qkv_back_call(
             load,

time: 1290 us -> 1260 us (0.977)
  Pallas kernels: 551 us -> 537 us
    pallas_call x4, Pallas kernels: 238 us -> 225 us  [ffn_call(): pl.pallas_call(kernel, grid=(experts,), in_specs=[pl.BlockSpec((1,) + hot...]
    unnamed x219 -> x234, local copies, waits for them, and re-layouts: 28 us -> 23.1 us
  transfers between devices with their start and end apart: 28 -> 28, of which waited for: 21 -> 20; matrix products, arithmetic and copies ran while one was open for 9% -> 9% of each run, Pallas kernels for 43% -> 43%
where the time goes in v1:
time: 1260 us; the launch traced here: 1250 us
  Pallas kernels  537 us (43%)
  waiting for transfers between devices  455 us (36%)
  other arithmetic  108 us (9%)
  local copies, waits for them, and re-layouts  80.2 us (6%)
  starting transfers between devices  28.5 us (2%)
  between operations  24.7 us (2%)
  matrix products  20.2 us (2%)
    pallas_call x4, Pallas kernels, ffn_call(): pl.pallas_call(kernel, grid=(experts,), in_specs=[pl.BlockSpec((1,) + hot...  225 us
    all_gather x7, waiting for transfers between devices, gather(): return lax.all_gather(values, 'shard', axis=0)  198 us
    reduce_scatter x6, waiting for transfers between devices, scatter(): return lax.psum_scatter(values, 'shard', scatter_dimension=0, tiled=True)  130 us
    ppermute x6, waiting for transfers between devices, cube_gather(): other = lax.ppermute(values, 'rep', [(k, k ^ bit) for k in range(reps)])  70.7 us
    pallas_call x4, Pallas kernels, rows_call(): pl.pallas_call(kernel, grid=(pairs,), in_specs=[by_pair(experts, slots, r...  56.3 us
    ppermute x9, waiting for transfers between devices, spread_blocks(): out.append(lax.ppermute(block(shard_id + hop), 'shard', pairs))  55.5 us
    pallas_call x2, Pallas kernels, qkv_back_call(): pl.pallas_call(kernel, grid=(total // (2 * rows),), in_specs=[pl.BlockSpe...  47 us
    pallas_call x2, Pallas kernels, qkv_call(): pl.pallas_call(functools.partial(qkv_kernel, span, tops, rank), grid=(sha...  45 us
  transfers between devices with their start and end apart: 28, of which 20 were waited for; matrix products, arithmetic and copies ran while one was open for 9% of the time, Pallas kernels for 43%

profile of v1, /device:TPU:0, one launch (start us, length us, event | category | flops | bytes accessed | tf_op | source)
XLA Modules:
  0.0 1252.8 jit_solution(9928035738432559527)
XLA Ops:
  21.3 5.1 collective-permute-start
  27.4 7.4 collective-permute-done
  34.9 30.1 %collective-permute-done.1 = bf16[4,64,512]{2,1,0:T(8,128)(2,1)} collective-permute-done((bf16[4,64,512]{2,1,0:T(8,128)(2,1)S(1)}, bf16[4,64,512]{2,1,0:T(8,128)(2,1)}, u32[]{:S(2)}, u32[]{:S(2)}) %collective-permute-start.1) | collective-permute-done | bytes 262176 | tf_op jit(solution)/shard_map/ppermute | solution.py:786
  68.9 20.4 %collective-permute-done.3 = bf16[4,64,2048]{2,1,0:T(8,128)(2,1)S(1)} collective-permute-done((bf16[4,64,2048]{2,1,0:T(8,128)(2,1)}, bf16[4,64,2048]{2,1,0:T(8,128)(2,1)S(1)}, u32[]{:S(2)}, u32[]{:S(2)}) %collective-permute-start.3) | collective-permute-done | bytes 1048608 | tf_op jit(solution)/shard_map/ppermute | solution.py:801
  92.6 41.9 %collective-permute-done.4 = bf16[4,2,64,2048]{3,2,1,0:T(8,128)(2,1)} collective-permute-done((bf16[4,2,64,2048]{3,2,1,0:T(8,128)(2,1)S(1)}, bf16[4,2,64,2048]{3,2,1,0:T(8,128)(2,1)}, u32[]{:S(2)}, u32[]{:S(2)}) %collective-permute-start.4) | collective-permute-done | bytes 2097184 | tf_op jit(solution)/shard_map/ppermute | solution.py:801
  134.5 2.4 select_bitcast_fusion.3
  137.0 2.6 pad_maximum_fusion.1
  139.7 36.2 %all-gather.19.cloned.1.call-done = bf16[1920,2048]{1,0:T(8,128)(2,1)} async-done(((bf16[480,2048]{1,0:T(8,128)(2,1)}), bf16[1920,2048]{1,0:T(8,128)(2,1)}) %all-gather.19.cloned.1.call-update) | async-done | bytes 7864336 | tf_op jit(solution)/shard_map/all_gather | solution.py:772
  183.1 5.5 select_bitcast_fusion.1
  188.7 8.2 pad_maximum_fusion
  202.5 24.5 %qkv.2 = (bf16[2,1024,512]{2,1,0:T(8,128)(2,1)}, bf16[1024,512]{1,0:T(8,128)(2,1)}, bf16[1024,512]{1,0:T(8,128)(2,1)}, bf16[1024,128]{1,0:T(8,128)(2,1)}) custom-call(bf16[4,480,2048]{2,1,0:T(8,128)(2,1)} %bitcast.447, bf16[4,448,128]{2,1,0:T(8,128)(2,1)} %pad.9.routes, bf16[4,2048,512]{2,1,0:T(8,128)(2,1)} %refs_5_.3, bf16[2,2048,512]{2,1,0:T(8,128)(2,1)} %refs_6_.3, ...), custom_call_target="tpu_custom_call" | custom-call | flops 12884901888 | bytes 20447232 | tf_op jit(solution)/shard_map/qkv/pallas_call | solution.py:169
  229.5 13.9 %attend_prompt.1 = (bf16[2,1024,512]{2,1,0:T(8,128)(2,1)S(1)}, f32[4,2,1024,1]{3,2,1,0:T(8,128)}) custom-call(bf16[2,1024,512]{2,1,0:T(8,128)(2,1)} %get-tuple-element.63.q, bf16[1024,512]{1,0:T(8,128)(2,1)S(1)} %copy-done.4, bf16[1024,512]{1,0:T(8,128)(2,1)S(1)} %copy-done.7), custom_call_target="tpu_custom_call" | custom-call | flops 2147483648 | bytes 8388608 | tf_op jit(solution)/shard_map/attend_prompt/pallas_call | solution.py:704
  244.7 16.3 %project_out.2 = bf16[1024,2048]{1,0:T(8,128)(2,1)} custom-call(bf16[1024,128]{1,0:T(8,128)(2,1)} %get-tuple-element.62.ext.refs_4_, bf16[2,1024,512]{2,1,0:T(8,128)(2,1)} %copy-done.10, bf16[4,512,2048]{2,1,0:T(8,128)(2,1)} %bitcast.364, bf16[16,512]{1,0:T(8,128)(2,1)} %dynamic-slice_bitcast_fusion.10.fac_a, bf16[16,2048]{1,0:T(8,128)(2,1)} %bitcast.436), custom_call_target="tpu_custom_call" | custom-call | flops 8589934592 | bytes 14680064 | tf_op jit(solution)/shard_map/project_out/pallas_call | solution.py:217
  264.0 4.5 broadcast_add_fusion.earlier
  268.6 20.6 %qkv.3 = (bf16[2,768,512]{2,1,0:T(8,128)(2,1)}, bf16[768,512]{1,0:T(8,128)(2,1)}, bf16[768,512]{1,0:T(8,128)(2,1)}, bf16[768,128]{1,0:T(8,128)(2,1)}) custom-call(bf16[4,480,2048]{2,1,0:T(8,128)(2,1)} %bitcast.448, bf16[4,448,128]{2,1,0:T(8,128)(2,1)} %pad.9.routes, bf16[4,2048,512]{2,1,0:T(8,128)(2,1)} %refs_5_.3, bf16[2,2048,512]{2,1,0:T(8,128)(2,1)} %refs_6_.3, ...), custom_call_target="tpu_custom_call" | custom-call | flops 9663676416 | bytes 20447232 | tf_op jit(solution)/shard_map/qkv/pallas_call | solution.py:169
  291.5 26.7 %attend_cont.1 = (bf16[2,768,512]{2,1,0:T(8,128)(2,1)S(1)}, f32[4,2,768,1]{3,2,1,0:T(8,128)}) custom-call(bf16[2,768,512]{2,1,0:T(8,128)(2,1)} %get-tuple-element.68.q, bf16[1024,512]{1,0:T(8,128)(2,1)S(1)} %copy-done.5, bf16[1024,512]{1,0:T(8,128)(2,1)S(1)} %copy-done.8, bf16[768,512]{1,0:T(8,128)(2,1)S(1)} %copy-done.11, bf16[768,512]{1,0:T(8,128)(2,1)S(1)} %copy-done.13, ...), custom_call_target="tpu_custom_call" | custom-call | flops 3221225472 | bytes 6291456 | tf_op jit(solution)/shard_map/attend_cont/pallas_call | solution.py:711
  319.4 13.4 %project_out.3 = bf16[768,2048]{1,0:T(8,128)(2,1)} custom-call(bf16[768,128]{1,0:T(8,128)(2,1)} %get-tuple-element.67.ext.refs_4_, bf16[2,768,512]{2,1,0:T(8,128)(2,1)} %copy-done.3, bf16[4,512,2048]{2,1,0:T(8,128)(2,1)} %bitcast.365, bf16[16,512]{1,0:T(8,128)(2,1)} %dynamic-slice_bitcast_fusion.10.fac_a, bf16[16,2048]{1,0:T(8,128)(2,1)} %bitcast.437), custom_call_target="tpu_custom_call" | custom-call | flops 6442450944 | bytes 13107200 | tf_op jit(solution)/shard_map/project_out/pallas_call | solution.py:217
  334.6 10.9 reduce-scatter.7.cloned.1.call-done
  354.3 85.7 %all-gather.13.cloned.1.call-done.refs_1_.refs_2_ = bf16[4,256,2176]{2,1,0:T(8,128)(2,1)} async-done(((bf16[1,256,2176]{2,1,0:T(8,128)(2,1)}), bf16[4,256,2176]{2,1,0:T(8,128)(2,1)}) %all-gather.13.cloned.1.call-update) | async-done | bytes 4456464 | tf_op jit(solution)/shard_map/all_gather | solution.py:772
  441.8 3.7 broadcast_add_fusion.2.refs_7_
  452.6 3.4 subtract_convert_fusion.4
  456.4 8.2 concatenate.154.refs_2_
  464.6 34.0 %ffn.4 = (bf16[1,544,2176]{2,1,0:T(8,128)(2,1)}, bf16[1,544,2176]{2,1,0:T(8,128)(2,1)}, f32[3,16,1408]{2,1,0:T(8,128)}) custom-call(bf16[4,2,272,512]{3,2,1,0:T(8,128)(2,1)} %fusion.refs_0_.hot, bf16[4,256,2176]{2,1,0:T(8,128)(2,1)} %all-gather.13.cloned.1.call-done.refs_1_.refs_2_, bf16[4,256,2176]{2,1,0:T(8,128)(2,1)} %concatenate.154.refs_2_, ...), custom_call_target="tpu_custom_call" | custom-call | flops 18824036352 | bytes 26214400 | tf_op jit(solution)/shard_map/ffn/pallas_call | solution.py:489
  500.5 3.9 reduce-scatter.9.cloned.1.call-done
  504.4 2.9 multiply_reduce_fusion.5
  515.6 91.5 %ffn.5 = (bf16[3,544,2176]{2,1,0:T(8,128)(2,1)}, bf16[3,544,2176]{2,1,0:T(8,128)(2,1)}, f32[3,16,1408]{2,1,0:T(8,128)}) custom-call(bf16[4,2,272,512]{3,2,1,0:T(8,128)(2,1)} %fusion.refs_0_.hot, bf16[4,256,2176]{2,1,0:T(8,128)(2,1)} %all-gather.13.cloned.1.call-done.refs_1_.refs_2_, bf16[4,256,2176]{2,1,0:T(8,128)(2,1)} %concatenate.154.refs_2_, ...), custom_call_target="tpu_custom_call" | custom-call | flops 56472109056 | bytes 78643200 | tf_op jit(solution)/shard_map/ffn/pallas_call | solution.py:489
  607.1 17.1 %slots_to_rows.4 = (bf16[1024,2176]{1,0:T(8,128)(2,1)}, f32[32,2048]{1,0:T(8,128)}) custom-call(bf16[4,2,272,512]{3,2,1,0:T(8,128)(2,1)} %fusion.refs_0_.hot, bf16[1,2,272,2176]{3,2,1,0:T(8,128)(2,1)} %bitcast.460, bf16[3,2,272,2176]{3,2,1,0:T(8,128)(2,1)} %bitcast.461, bf16[4,256,2176]{2,1,0:T(8,128)(2,1)} %all-gather.13.cloned.1.call-done.refs_1_.refs_2_, ...), custom_call_target="tpu_custom_call" | custom-call | flops 4848615424 | bytes 11698176 | tf_op jit(solution)/shard_map/slots_to_rows/pallas_call | solution.py:556
  626.5 18.6 %slots_to_rows.5 = (bf16[1024,2048]{1,0:T(8,128)(2,1)}, f32[16,2048]{1,0:T(8,128)}) custom-call(bf16[4,2,272,512]{3,2,1,0:T(8,128)(2,1)} %fusion.refs_0_.hot, bf16[1,2,272,2176]{3,2,1,0:T(8,128)(2,1)} %bitcast.379, bf16[3,2,272,2176]{3,2,1,0:T(8,128)(2,1)} %bitcast.368, bf16[4,256,2176]{2,1,0:T(8,128)(2,1)} %concatenate.154.refs_2_, ...), custom_call_target="tpu_custom_call" | custom-call | flops 4848615424 | bytes 11698176 | tf_op jit(solution)/shard_map/slots_to_rows/pallas_call | solution.py:556
  645.1 2.8 subtract_convert_fusion.5
  648.3 6.1 concatenate.170.refs_2_
  654.4 49.5 %ffn.6 = (bf16[2,416,2176]{2,1,0:T(8,128)(2,1)}, bf16[2,416,2176]{2,1,0:T(8,128)(2,1)}, f32[3,16,1408]{2,1,0:T(8,128)}) custom-call(bf16[4,2,208,384]{3,2,1,0:T(8,128)(2,1)} %fusion.5.refs_0_.hot, bf16[4,192,2176]{2,1,0:T(8,128)(2,1)} %all-gather.15.cloned.1.call-done.refs_1_.refs_2_, bf16[4,192,2176]{2,1,0:T(8,128)(2,1)} %concatenate.170.refs_2_, ...), custom_call_target="tpu_custom_call" | custom-call | flops 28789702656 | bytes 48234496 | tf_op jit(solution)/shard_map/ffn/pallas_call | solution.py:489
  705.7 17.5 %reduce-scatter.11.cloned.1.call-done = bf16[256,2176]{1,0:T(8,128)(2,1)} async-done(((bf16[1024,2176]{1,0:T(8,128)(2,1)}), bf16[256,2176]{1,0:T(8,128)(2,1)}) %reduce-scatter.11.cloned.1.call-update) | async-done | bytes 1114128 | tf_op jit(solution)/shard_map/reduce_scatter | solution.py:775
  724.4 3.2 multiply_reduce_fusion.1
  730.8 49.6 %ffn.7 = (bf16[2,416,2176]{2,1,0:T(8,128)(2,1)}, bf16[2,416,2176]{2,1,0:T(8,128)(2,1)}, f32[3,16,1408]{2,1,0:T(8,128)}) custom-call(bf16[4,2,208,384]{3,2,1,0:T(8,128)(2,1)} %fusion.5.refs_0_.hot, bf16[4,192,2176]{2,1,0:T(8,128)(2,1)} %all-gather.15.cloned.1.call-done.refs_1_.refs_2_, bf16[4,192,2176]{2,1,0:T(8,128)(2,1)} %concatenate.170.refs_2_, ...), custom_call_target="tpu_custom_call" | custom-call | flops 28789702656 | bytes 48234496 | tf_op jit(solution)/shard_map/ffn/pallas_call | solution.py:489
  780.4 10.5 slots_to_rows.6
  790.9 21.3 %all-gather.21.cloned.1.call-done = bf16[1024,2048]{1,0:T(8,128)(2,1)} async-done(((bf16[256,2048]{1,0:T(8,128)(2,1)}), bf16[1024,2048]{1,0:T(8,128)(2,1)}) %all-gather.21.cloned.1.call-update) | async-done | bytes 4194320 | tf_op jit(solution)/shard_map/all_gather | solution.py:772
  814.0 3.9 broadcast_add_fusion.1
  818.1 20.3 %project_out_back.2 = (bf16[2,1024,512]{2,1,0:T(8,128)(2,1)}, bf16[1024,128]{1,0:T(8,128)(2,1)}, f32[16,512]{1,0:T(8,128)}, f32[16,2048]{1,0:T(8,128)}) custom-call(bf16[1024,128]{1,0:T(8,128)(2,1)} %get-tuple-element.62.ext.refs_4_, bf16[4,256,2048]{2,1,0:T(8,128)(2,1)} %bitcast.457, bf16[2,1024,512]{2,1,0:T(8,128)(2,1)} %copy-done.10, ...), custom_call_target="tpu_custom_call" | custom-call | flops 8589934592 | bytes 16777216 | tf_op jit(solution)/shard_map/project_out_back/pallas_call | solution.py:277
  838.4 23.8 %attend_prompt_back.1 = (bf16[2,1024,512]{2,1,0:T(8,128)(2,1)S(1)}, f32[1024,512]{1,0:T(8,128)}, f32[1024,512]{1,0:T(8,128)}) custom-call(bf16[2,1024,512]{2,1,0:T(8,128)(2,1)} %get-tuple-element.63.q, bf16[1024,512]{1,0:T(8,128)(2,1)S(1)} %copy-done.6, bf16[1024,512]{1,0:T(8,128)(2,1)S(1)} %copy-done.9, bf16[2,1024,512]{2,1,0:T(8,128)(2,1)} %get-tuple-element.84.do, ...), custom_call_target="tpu_custom_call" | custom-call | flops 6442450944 | bytes 8388608 | tf_op jit(solution)/shard_map/attend_prompt_back/pallas_call | solution.py:718
  863.5 16.5 %reduce-scatter.13.cloned.1.call-done = bf16[192,2176]{1,0:T(8,128)(2,1)} async-done(((bf16[768,2176]{1,0:T(8,128)(2,1)}), bf16[192,2176]{1,0:T(8,128)(2,1)}) %reduce-scatter.13.cloned.1.call-update) | async-done | bytes 835600 | tf_op jit(solution)/shard_map/reduce_scatter | solution.py:775
  881.1 3.2 multiply_reduce_fusion.4
  887.1 10.1 slots_to_rows.7
  897.2 53.7 %all-gather.23.cloned.1.call-done = bf16[768,2048]{1,0:T(8,128)(2,1)} async-done(((bf16[192,2048]{1,0:T(8,128)(2,1)}), bf16[768,2048]{1,0:T(8,128)(2,1)}) %all-gather.23.cloned.1.call-update) | async-done | bytes 3145744 | tf_op jit(solution)/shard_map/all_gather | solution.py:772
  952.7 8.9 maximum_add_fusion
  961.7 16.8 %project_out_back.3 = (bf16[2,768,512]{2,1,0:T(8,128)(2,1)}, bf16[768,128]{1,0:T(8,128)(2,1)}, f32[16,512]{1,0:T(8,128)}, f32[16,2048]{1,0:T(8,128)}) custom-call(bf16[768,128]{1,0:T(8,128)(2,1)} %get-tuple-element.67.ext.refs_4_, bf16[4,192,2048]{2,1,0:T(8,128)(2,1)} %bitcast.459, bf16[2,768,512]{2,1,0:T(8,128)(2,1)} %copy-done.3, ...), custom_call_target="tpu_custom_call" | custom-call | flops 6442450944 | bytes 14680064 | tf_op jit(solution)/shard_map/project_out_back/pallas_call | solution.py:277
  978.6 33.0 %attend_cont_back.1 = (bf16[2,768,512]{2,1,0:T(8,128)(2,1)}, bf16[1024,512]{1,0:T(8,128)(2,1)S(1)}, bf16[1024,512]{1,0:T(8,128)(2,1)S(1)}, bf16[768,512]{1,0:T(8,128)(2,1)S(1)}, bf16[768,512]{1,0:T(8,128)(2,1)S(1)}) custom-call(bf16[2,768,512]{2,1,0:T(8,128)(2,1)} %get-tuple-element.68.q, bf16[1024,512]{1,0:T(8,128)(2,1)} %get-tuple-element.64.k.kp, ...), custom_call_target="tpu_custom_call" | custom-call | flops 9663676416 | bytes 6291456 | tf_op jit(solution)/shard_map/attend_cont_back/pallas_call | solution.py:725
  1015.2 25.6 %qkv_back.2 = (bf16[1024,2048]{1,0:T(8,128)(2,1)}, f32[48,2048]{1,0:T(8,128)}, f32[3,16,512]{2,1,0:T(8,128)}) custom-call(bf16[4,480,2048]{2,1,0:T(8,128)(2,1)} %bitcast.449, bf16[2,1024,512]{2,1,0:T(8,128)(2,1)} %copy-done.2, bf16[1024,512]{1,0:T(8,128)(2,1)} %copy-done.17, bf16[1024,512]{1,0:T(8,128)(2,1)} %copy-done.18, ...), custom_call_target="tpu_custom_call" | custom-call | flops 12884901888 | bytes 28311552 | tf_op jit(solution)/shard_map/qkv_back/pallas_call | solution.py:348
  1040.8 21.4 %qkv_back.3 = (bf16[768,2048]{1,0:T(8,128)(2,1)}, f32[48,2048]{1,0:T(8,128)}, f32[3,16,512]{2,1,0:T(8,128)}) custom-call(bf16[4,480,2048]{2,1,0:T(8,128)(2,1)} %bitcast.450, bf16[2,768,512]{2,1,0:T(8,128)(2,1)} %get-tuple-element.94.refs_1_, bf16[768,512]{1,0:T(8,128)(2,1)} %copy-done.15, bf16[768,512]{1,0:T(8,128)(2,1)} %copy-done.16, ...), custom_call_target="tpu_custom_call" | custom-call | flops 9663676416 | bytes 28311552 | tf_op jit(solution)/shard_map/qkv_back/pallas_call | solution.py:348
  1062.3 26.0 %reduce-scatter.15.cloned.1.call-done = bf16[448,2048]{1,0:T(8,128)(2,1)} async-done(((bf16[1792,2048]{1,0:T(8,128)(2,1)}), bf16[448,2048]{1,0:T(8,128)(2,1)}) %reduce-scatter.15.cloned.1.call-update) | async-done | bytes 1835024 | tf_op jit(solution)/shard_map/reduce_scatter | solution.py:775
  1090.1 9.0 maximum_add_fusion.1
  1104.1 3.0 collective-permute-start.10
  1109.1 14.1 %collective-permute-done.10 = bf16[112,512]{1,0:T(8,128)(2,1)S(1)} collective-permute-done((bf16[112,512]{1,0:T(8,128)(2,1)S(1)}, bf16[112,512]{1,0:T(8,128)(2,1)S(1)}, u32[]{:S(2)}, u32[]{:S(2)}) %collective-permute-start.10) | collective-permute-done | bytes 114720 | tf_op jit(solution)/shard_map/ppermute | solution.py:786
  1126.1 6.4 collective-permute-done.12
  1134.7 7.9 collective-permute-start.6
  1142.6 2.4 collective-permute-start.8
  1147.3 3.3 collective-permute-done.7
  1151.9 10.1 multiply_reduce_fusion
  1169.6 2.8 reshape.667
  1172.4 2.7 slice.309
  1179.6 55.4 %reduce-scatter.17.cloned.1.call-done = bf16[448,2048]{1,0:T(8,128)(2,1)} async-done(((bf16[1792,2048]{1,0:T(8,128)(2,1)}), bf16[448,2048]{1,0:T(8,128)(2,1)}) %reduce-scatter.17.cloned.1.call-update) | async-done | bytes 1835024 | tf_op jit(solution)/shard_map/reduce_scatter | solution.py:775
  1235.0 2.4 multiply_reduce_fusion.3
  1237.5 2.8 fusion.13
  1240.5 2.5 subtract_add_fusion
  1243.0 3.0 fusion.12
  (489 shorter events, 117.1 us)
Async XLA Ops:
  7.2 439.5 %copy-start = (bf16[8,16,1408]{2,1,0:T(8,128)(2,1)S(1)}, bf16[8,16,1408]{2,1,0:T(8,128)(2,1)}, u32[]{:S(2)}) copy-start(bf16[8,16,1408]{2,1,0:T(8,128)(2,1)} %param.40) | copy-start | bytes 1081348
  7.2 8.4 copy-start.19
  7.2 8.0 copy-start.21
  7.2 168.7 %all-gather.19.cloned.1.call-start = ((), (), s32[]{:S(2)}) async-start(), calls=%async_computation.16 | async-start | bytes 9830400 | tf_op jit(solution)/shard_map/all_gather | solution.py:772
  8.1 7.8 copy-start.68
  10.2 5.7 copy-start.96
  13.3 498.2 %copy-start.77 = (s32[192,2]{0,1:T(2,128)}, s32[192,2]{0,1:T(2,128)S(1)}, u32[]{:S(2)}) copy-start(s32[192,2]{0,1:T(2,128)S(1)} %reshape_squeeze.9) | copy-start | bytes 4612
  18.7 243.5 %all-gather.11.cloned.1.call-start = ((), (), s32[]{:S(2)}) async-start(), calls=%async_computation.6 | async-start | bytes 5242880 | tf_op jit(solution)/shard_map/all_gather | solution.py:772
  21.3 13.6 %collective-permute-start = (bf16[4,64,512]{2,1,0:T(8,128)(2,1)S(1)}, bf16[4,64,512]{2,1,0:T(8,128)(2,1)S(1)}, u32[]{:S(2)}, u32[]{:S(2)}) collective-permute-start(bf16[4,64,512]{2,1,0:T(8,128)(2,1)S(1)} %get-tuple-element.158), channel_id=1, source_target_pairs={{0,3},{1,0},{2,1},{3,2},{4,7},{5,4},{6,5},{7,6},{8,11},{9,8},{10,9... | collective-permute-start | bytes 786440 | tf_op jit(solution)/shard_map/ppermute | solution.py:786
  26.4 38.6 %collective-permute-start.1 = (bf16[4,64,512]{2,1,0:T(8,128)(2,1)S(1)}, bf16[4,64,512]{2,1,0:T(8,128)(2,1)}, u32[]{:S(2)}, u32[]{:S(2)}) collective-permute-start(bf16[4,64,512]{2,1,0:T(8,128)(2,1)S(1)} %get-tuple-element.157), channel_id=1, source_target_pairs={{0,2},{1,3},{2,0},{3,1},{4,6},{5,7},{6,4},{7,5},{8,10},{9,11},{10,... | collective-permute-start | bytes 786440 | tf_op jit(solution)/shard_map/ppermute | solution.py:786
  26.4 38.6 %collective-permute-start.2 = (bf16[4,64,512]{2,1,0:T(8,128)(2,1)S(1)}, bf16[4,64,512]{2,1,0:T(8,128)(2,1)}, u32[]{:S(2)}, u32[]{:S(2)}) collective-permute-start(bf16[4,64,512]{2,1,0:T(8,128)(2,1)S(1)} %get-tuple-element.156), channel_id=1, source_target_pairs={{0,1},{1,2},{2,3},{3,0},{4,5},{5,6},{6,7},{7,4},{8,9},{9,10},{10,1... | collective-permute-start | bytes 786440 | tf_op jit(solution)/shard_map/ppermute | solution.py:786
  34.9 30.1 %copy-start.67 = (bf16[4,64,512]{2,1,0:T(8,128)(2,1)}, bf16[4,64,512]{2,1,0:T(8,128)(2,1)S(1)}, u32[]{:S(2)}) copy-start(bf16[4,64,512]{2,1,0:T(8,128)(2,1)S(1)} %collective-permute-done) | copy-start | bytes 786436
  67.4 21.9 %collective-permute-start.3 = (bf16[4,64,2048]{2,1,0:T(8,128)(2,1)}, bf16[4,64,2048]{2,1,0:T(8,128)(2,1)S(1)}, u32[]{:S(2)}, u32[]{:S(2)}) collective-permute-start(bf16[4,64,2048]{2,1,0:T(8,128)(2,1)} %pad_maximum_fusion.8), channel_id=1, source_target_pairs={{0,16},{4,20},{8,24},{12,28},{16,0},{20,4},{24,8},{28,12},{1,17},{... | collective-permute-start | bytes 3145736 | tf_op jit(solution)/shard_map/ppermute | solution.py:801
  91.1 43.4 %collective-permute-start.4 = (bf16[4,2,64,2048]{3,2,1,0:T(8,128)(2,1)S(1)}, bf16[4,2,64,2048]{3,2,1,0:T(8,128)(2,1)}, u32[]{:S(2)}, u32[]{:S(2)}) collective-permute-start(bf16[4,2,64,2048]{3,2,1,0:T(8,128)(2,1)S(1)} %pad_maximum_fusion.3), channel_id=1, source_target_pairs={{0,8},{4,12},{8,0},{12,4},{16,24},{20,28},{24,16},{28,20},{1,9},{5... | collective-permute-start | bytes 6291464 | tf_op jit(solution)/shard_map/ppermute | solution.py:801
  139.7 43.5 %collective-permute-start.5 = (bf16[4,2,2,64,2048]{4,3,2,1,0:T(8,128)(2,1)}, bf16[4,2,2,64,2048]{4,3,2,1,0:T(8,128)(2,1)}, u32[]{:S(2)}, u32[]{:S(2)}) collective-permute-start(bf16[4,2,2,64,2048]{4,3,2,1,0:T(8,128)(2,1)} %pad_maximum_fusion.1), channel_id=1, source_target_pairs={{0,4},{4,0},{8,12},{12,8},{16,20},{20,16},{24,28},{28,24},{1,5},{5... | collective-permute-start | bytes 12582920 | tf_op jit(solution)/shard_map/ppermute | solution.py:801
  180.0 165.4 %reduce-scatter.7.cloned.1.call-start = ((), (), s32[]{:S(2)}) async-start(), calls=%async_computation.7 | async-start | bytes 5242880 | tf_op jit(solution)/shard_map/reduce_scatter | solution.py:775
  198.7 28.3 %copy-start.55 = (bf16[6,8,4,512]{3,1,2,0:T(8,128)(2,1)}, bf16[6,8,4,512]{3,1,2,0:T(8,128)(2,1)S(1)}, u32[]{:S(2)}) copy-start(bf16[6,8,4,512]{3,1,2,0:T(8,128)(2,1)S(1)} %copy.337) | copy-start | bytes 589828
  268.5 171.5 %all-gather.13.cloned.1.call-start = ((), (), s32[]{:S(2)}) async-start(), calls=%async_computation.8 | async-start | bytes 5570560 | tf_op jit(solution)/shard_map/all_gather | solution.py:772
  268.6 79.7 %copy-start.50 = (bf16[4,8,4,512]{3,1,2,0:T(8,128)(2,1)}, bf16[4,8,4,512]{3,1,2,0:T(8,128)(2,1)S(1)}, u32[]{:S(2)}) copy-start(bf16[4,8,4,512]{3,1,2,0:T(8,128)(2,1)S(1)} %copy.339) | copy-start | bytes 393220
  268.6 20.6 %copy-start.5 = (bf16[1024,512]{1,0:T(8,128)(2,1)S(1)}, bf16[1024,512]{1,0:T(8,128)(2,1)}, u32[]{:S(2)}) copy-start(bf16[1024,512]{1,0:T(8,128)(2,1)} %get-tuple-element.64.k.kp) | copy-start | bytes 3145732
  268.6 20.6 %copy-start.8 = (bf16[1024,512]{1,0:T(8,128)(2,1)S(1)}, bf16[1024,512]{1,0:T(8,128)(2,1)}, u32[]{:S(2)}) copy-start(bf16[1024,512]{1,0:T(8,128)(2,1)} %get-tuple-element.65.v.vp) | copy-start | bytes 3145732
  347.8 379.9 %copy-start.87 = (f32[256]{0:T(256)}, f32[256]{0:T(256)S(1)}, u32[]{:S(2)}) copy-start(f32[256]{0:T(256)S(1)} %get-tuple-element.186) | copy-start | bytes 3076
  354.2 150.2 %reduce-scatter.9.cloned.1.call-start = ((), (), s32[]{:S(2)}) async-start(), calls=%async_computation.9 | async-start | bytes 3932160 | tf_op jit(solution)/shard_map/reduce_scatter | solution.py:775
  445.5 199.6 %all-gather.17.cloned.1.call-start = ((), (), s32[]{:S(2)}) async-start(), calls=%async_computation.11 | async-start | bytes 3932160 | tf_op jit(solution)/shard_map/all_gather | solution.py:772
  450.3 5.7 copy-start.53
  498.6 9.3 copy-start.22
  510.4 144.1 %all-gather.15.cloned.1.call-start = ((), (), s32[]{:S(2)}) async-start(), calls=%async_computation.10 | async-start | bytes 4177920 | tf_op jit(solution)/shard_map/all_gather | solution.py:772
  515.6 207.6 %reduce-scatter.11.cloned.1.call-start = ((), (), s32[]{:S(2)}) async-start(), calls=%async_computation.12 | async-start | bytes 5570560 | tf_op jit(solution)/shard_map/reduce_scatter | solution.py:775
  624.2 188.0 %all-gather.21.cloned.1.call-start = ((), (), s32[]{:S(2)}) async-start(), calls=%async_computation.17 | async-start | bytes 5242880 | tf_op jit(solution)/shard_map/all_gather | solution.py:772
  626.5 18.7 %copy-start.54 = (bf16[2,8,4,512]{3,1,2,0:T(8,128)(2,1)S(1)}, bf16[2,8,4,512]{3,1,2,0:T(8,128)(2,1)}, u32[]{:S(2)}) copy-start(bf16[2,8,4,512]{3,1,2,0:T(8,128)(2,1)} %copy-done.53) | copy-start | bytes 196612
  730.8 149.2 %reduce-scatter.13.cloned.1.call-start = ((), (), s32[]{:S(2)}) async-start(), calls=%async_computation.13 | async-start | bytes 4177920 | tf_op jit(solution)/shard_map/reduce_scatter | solution.py:775
  818.0 20.4 %copy-start.6 = (bf16[1024,512]{1,0:T(8,128)(2,1)S(1)}, bf16[1024,512]{1,0:T(8,128)(2,1)}, u32[]{:S(2)}) copy-start(bf16[1024,512]{1,0:T(8,128)(2,1)} %get-tuple-element.64.k.kp) | copy-start | bytes 3145732
  818.0 132.9 %all-gather.23.cloned.1.call-start = ((), (), s32[]{:S(2)}) async-start(), calls=%async_computation.18 | async-start | bytes 3932160 | tf_op jit(solution)/shard_map/all_gather | solution.py:772
  818.1 20.3 %copy-start.9 = (bf16[1024,512]{1,0:T(8,128)(2,1)S(1)}, bf16[1024,512]{1,0:T(8,128)(2,1)}, u32[]{:S(2)}) copy-start(bf16[1024,512]{1,0:T(8,128)(2,1)} %get-tuple-element.65.v.vp) | copy-start | bytes 3145732
  838.4 42.5 %copy-start.78 = (s32[192,2]{0,1:T(2,128)S(1)}, s32[192,2]{0,1:T(2,128)}, u32[]{:S(2)}) copy-start(s32[192,2]{0,1:T(2,128)} %copy-done.77) | copy-start | bytes 4612
  838.4 42.6 %copy-start.76 = (f32[192,2]{0,1:T(2,128)S(1)}, f32[192,2]{0,1:T(2,128)}, u32[]{:S(2)}) copy-start(f32[192,2]{0,1:T(2,128)} %copy-done.75) | copy-start | bytes 4612
  838.4 42.6 %copy-start.85 = (f32[192]{0:T(256)S(1)}, f32[192]{0:T(256)}, u32[]{:S(2)}) copy-start(f32[192]{0:T(256)} %copy-done.84) | copy-start | bytes 2308
  838.4 42.6 %copy-start.93 = (f32[192]{0:T(256)S(1)}, f32[192]{0:T(256)}, u32[]{:S(2)}) copy-start(f32[192]{0:T(256)} %copy-done.92) | copy-start | bytes 2308
  862.2 22.1 %copy-start.2 = (bf16[2,1024,512]{2,1,0:T(8,128)(2,1)}, bf16[2,1024,512]{2,1,0:T(8,128)(2,1)S(1)}, u32[]{:S(2)}) copy-start(bf16[2,1024,512]{2,1,0:T(8,128)(2,1)S(1)} %get-tuple-element.86.refs_1_) | copy-start | bytes 6291460
  887.1 201.1 %reduce-scatter.15.cloned.1.call-start = ((), (), s32[]{:S(2)}) async-start(), calls=%async_computation.14 | async-start | bytes 9175040 | tf_op jit(solution)/shard_map/reduce_scatter | solution.py:775
  961.7 16.9 %copy-start.12 = (bf16[768,512]{1,0:T(8,128)(2,1)S(1)}, bf16[768,512]{1,0:T(8,128)(2,1)}, u32[]{:S(2)}) copy-start(bf16[768,512]{1,0:T(8,128)(2,1)} %get-tuple-element.69.k) | copy-start | bytes 2359300
  961.7 16.9 %copy-start.14 = (bf16[768,512]{1,0:T(8,128)(2,1)S(1)}, bf16[768,512]{1,0:T(8,128)(2,1)}, u32[]{:S(2)}) copy-start(bf16[768,512]{1,0:T(8,128)(2,1)} %get-tuple-element.70.v) | copy-start | bytes 2359300
  961.7 273.3 %reduce-scatter.17.cloned.1.call-start = ((), (), s32[]{:S(2)}) async-start(), calls=%async_computation.15 | async-start | bytes 9175040 | tf_op jit(solution)/shard_map/reduce_scatter | solution.py:775
  1100.8 8.3 copy-start.80
  1100.8 8.3 copy-start.81
  1103.9 21.8 %copy-start.83 = (s32[192,2]{0,1:T(2,128)S(1)}, s32[192,2]{0,1:T(2,128)}, u32[]{:S(2)}) copy-start(s32[192,2]{0,1:T(2,128)} %copy-done.82) | copy-start | bytes 4612
  1103.9 21.8 %copy-start.43 = (bf16[256,2048]{1,0:T(8,128)(2,1)S(1)}, bf16[256,2048]{1,0:T(8,128)(2,1)}, u32[]{:S(2)}) copy-start(bf16[256,2048]{1,0:T(8,128)(2,1)} %copy-done.42) | copy-start | bytes 3145732
  1104.1 19.2 %collective-permute-start.10 = (bf16[112,512]{1,0:T(8,128)(2,1)S(1)}, bf16[112,512]{1,0:T(8,128)(2,1)S(1)}, u32[]{:S(2)}, u32[]{:S(2)}) collective-permute-start(bf16[112,512]{1,0:T(8,128)(2,1)S(1)} %get-tuple-element.165), channel_id=1, source_target_pairs={{0,2},{1,3},{2,0},{3,1},{4,6},{5,7},{6,4},{7,5},{8,10},{9,11},{10,... | collective-permute-start | bytes 344072 | tf_op jit(solution)/shard_map/ppermute | solution.py:786
  1107.1 16.7 %collective-permute-start.11 = (bf16[112,512]{1,0:T(8,128)(2,1)S(1)}, bf16[112,512]{1,0:T(8,128)(2,1)S(1)}, u32[]{:S(2)}, u32[]{:S(2)}) collective-permute-start(bf16[112,512]{1,0:T(8,128)(2,1)S(1)} %get-tuple-element.164), channel_id=1, source_target_pairs={{0,3},{1,0},{2,1},{3,2},{4,7},{5,4},{6,5},{7,6},{8,11},{9,8},{10,9... | collective-permute-start | bytes 344072 | tf_op jit(solution)/shard_map/ppermute | solution.py:786
  1108.0 15.8 %collective-permute-start.9 = (bf16[112,512]{1,0:T(8,128)(2,1)S(1)}, bf16[112,512]{1,0:T(8,128)(2,1)S(1)}, u32[]{:S(2)}, u32[]{:S(2)}) collective-permute-start(bf16[112,512]{1,0:T(8,128)(2,1)S(1)} %get-tuple-element.163), channel_id=1, source_target_pairs={{0,1},{1,2},{2,3},{3,0},{4,5},{5,6},{6,7},{7,4},{8,9},{9,10},{10,1... | collective-permute-start | bytes 344072 | tf_op jit(solution)/shard_map/ppermute | solution.py:786
  1124.0 10.2 copy-start.86
  1124.0 10.3 copy-start.95
  1124.0 10.3 copy-start.65
  1124.1 10.4 copy-start.70
  1124.1 8.3 collective-permute-start.12
  1132.6 14.4 %collective-permute-start.13 = (bf16[2,1248,128]{2,1,0:T(8,128)(2,1)S(1)}, bf16[2,1248,128]{2,1,0:T(8,128)(2,1)S(1)}, u32[]{:S(2)}, u32[]{:S(2)}) collective-permute-start(bf16[2,1248,128]{2,1,0:T(8,128)(2,1)S(1)} %pad_maximum_fusion.10), channel_id=1, source_target_pairs={{0,8},{4,12},{8,0},{12,4},{16,24},{20,28},{24,16},{28,20},{1,9},{5... | collective-permute-start | bytes 1916936 | tf_op jit(solution)/shard_map/ppermute | solution.py:801
  1134.7 12.7 %collective-permute-start.6 = (bf16[2,448]{1,0:T(2,128)(2,1)S(1)}, bf16[2,448]{1,0:T(2,128)(2,1)S(1)}, u32[]{:S(2)}, u32[]{:S(2)}) collective-permute-start(bf16[2,448]{1,0:T(2,128)(2,1)S(1)} %get-tuple-element.176), channel_id=1, source_target_pairs={{0,1},{1,2},{2,3},{3,0},{4,5},{5,6},{6,7},{7,4},{8,9},{9,10},{10,1... | collective-permute-start | bytes 5384 | tf_op jit(solution)/shard_map/ppermute | solution.py:786
  1142.6 8.1 collective-permute-start.7
  1142.6 8.1 collective-permute-start.8
  1147.2 3.5 collective-permute-start.14
  1176.3 58.7 %copy-start.35 = (f32[192,2048]{1,0:T(8,128)S(1)}, f32[192,2048]{1,0:T(8,128)}, u32[]{:S(2)}) copy-start(f32[192,2048]{1,0:T(8,128)} %get-tuple-element.131) | copy-start | bytes 4718596
  1176.3 58.7 %copy-start.69 = (f32[1,2048]{1,0:T(1,128)S(1)}, f32[1,2048]{1,0:T(1,128)}, u32[]{:S(2)}) copy-start(f32[1,2048]{1,0:T(1,128)} %copy-done.68) | copy-start | bytes 24580
  1179.6 57.8 %copy-start.20 = (bf16[1,256,2048]{2,1,0:T(8,128)(2,1)S(1)}, bf16[1,256,2048]{2,1,0:T(8,128)(2,1)}, u32[]{:S(2)}) copy-start(bf16[1,256,2048]{2,1,0:T(8,128)(2,1)} %param.21) | copy-start | bytes 3145732
  1235.0 5.3 copy-start.52
  (72 other events, 177.9 us)
Sparse Core Ops, SparseCore 0:
  18.8 157.0 all-gather.18
  180.2 81.9 all-gather.10
  268.6 76.8 reduce-scatter.6
  354.4 85.5 all-gather.12
  445.7 58.7 reduce-scatter.8
  510.5 63.5 all-gather.16
  575.7 65.3 all-gather.14
  643.5 79.6 reduce-scatter.10
  730.9 81.2 all-gather.20
  818.1 61.8 reduce-scatter.12
  887.2 63.6 all-gather.22
  961.8 126.3 reduce-scatter.14
  1099.2 135.7 reduce-scatter.16
